TPU v7x, 32 devices: a whole 2x2x4 slice. The times are simulated.
32 devices in a mesh: ctx: 8 (over y, x, core), shard: 4 (over z).
Axes of the slice: x: 2, y: 2, z: 4, core: 2. Of those that a mesh axis runs over, the one named last changes fastest.
Arguments:
- layer_input: bfloat16 [4, 1024, 2048], P('shard', 'ctx'), may hold values from -6 to 6
- out_grad: bfloat16 [4, 1024, 2048], P('shard', 'ctx'), may hold values from -6 to 6
- positions: int32 [4, 1024], P('shard'), may hold values from 0 to 1023, as said below
- w_qkv: float32 [2048, 6144], P(('ctx', 'shard')), may hold values from -0.1875 to 0.1875
- w_dense: float32 [2048, 2048], P(('ctx', 'shard')), may hold values from -0.75 to 0.75
- w_up: float32 [2048, 8192], P(('ctx', 'shard')), may hold values from -0.125 to 0.125
- w_down: float32 [8192, 2048], P(('ctx', 'shard')), may hold values from -0.0625 to 0.0625
- vectors: float32 [13, 2048], P(None, ('ctx', 'shard')), may hold values from -0.6 to 1.3
- m_qkv: float32 [2048, 6144], P(('ctx', 'shard')), may hold values from -128 to 128
- m_dense: float32 [2048, 2048], P(('ctx', 'shard')), may hold values from -8 to 8
- m_up: float32 [2048, 8192], P(('ctx', 'shard')), may hold values from -10 to 10
- m_down: float32 [8192, 2048], P(('ctx', 'shard')), may hold values from -20 to 20
- m_vectors: float32 [13, 2048], P(None, ('ctx', 'shard')), may hold values from -80 to 80
- v_qkv: float32 [2048, 6144], P(('ctx', 'shard')), may hold values from 970.752 to 15523.84
- v_dense: float32 [2048, 2048], P(('ctx', 'shard')), may hold values from 4.3008 to 68.8128
- v_up: float32 [2048, 8192], P(('ctx', 'shard')), may hold values from 6.71744 to 107.7248
- v_down: float32 [8192, 2048], P(('ctx', 'shard')), may hold values from 27.0336 to 430.08
- v_vectors: float32 [13, 2048], P(None, ('ctx', 'shard')), may hold values from 430.08 to 6881.28
Outputs:
- layer_output: bfloat16 [4, 1024, 2048], P('shard', 'ctx')
- grad_input: float32 [4, 1024, 2048], P('shard', 'ctx')
- grad_qkv: float32 [2048, 6144], P(('ctx', 'shard'))
- grad_dense: float32 [2048, 2048], P(('ctx', 'shard'))
- grad_up: float32 [2048, 8192], P(('ctx', 'shard'))
- grad_down: float32 [8192, 2048], P(('ctx', 'shard'))
- grad_vectors: float32 [13, 2048], P(None, ('ctx', 'shard'))
- second_qkv: float32 [2048, 6144], P(('ctx', 'shard'))
- second_dense: float32 [2048, 2048], P(('ctx', 'shard'))
- second_up: float32 [2048, 8192], P(('ctx', 'shard'))
- second_down: float32 [8192, 2048], P(('ctx', 'shard'))
- second_vectors: float32 [13, 2048], P(None, ('ctx', 'shard'))
- new_qkv: float32 [2048, 6144], P(('ctx', 'shard'))
- new_dense: float32 [2048, 2048], P(('ctx', 'shard'))
- new_up: float32 [2048, 8192], P(('ctx', 'shard'))
- new_down: float32 [8192, 2048], P(('ctx', 'shard'))
- new_vectors: float32 [13, 2048], P(None, ('ctx', 'shard'))
Inputs may be any that keep to these rules, and one draw needn't show every extreme that they name: `positions`: each sequence holds every place once; stored rows k * 128 to (k + 1) * 128 - 1 hold 128 rising places that begin at a multiple of 128.
All inputs are finite; a program needn't handle non-finite values.
Results may differ from a plain program's by a relative error of at most 0.012.
The roundings to bfloat16 on the way count: a program that leaves them out, or rounds other values in their place, can miss the bound.
Values may be sent and summed in bfloat16 or wider, within the bound.
A program may use at most 640 MiB of HBM per device.

v0:
```python
from functools import partial

import jax
import jax.numpy as jnp
from jax import lax
from jax.experimental import pallas as pl
from jax.experimental.pallas import tpu as pltpu
from jax.sharding import Mesh, PartitionSpec as P

D = 2048
H = 8
HD = 256
ROT = 64
FF = 8192
STEP = 10


def from_behind(value, axis, steps):
    count = lax.axis_size(axis)
    pairs = [(source, (source + steps) % count) for source in range(count)]
    return lax.ppermute(value, axis, pairs)


def layer_norm(values, gain, shift):
    center = values - jnp.mean(values, axis=-1, keepdims=True)
    spread = jnp.mean(center * center, axis=-1, keepdims=True)
    return center * lax.rsqrt(spread + 1e-05) * gain + shift


def angles(places):
    inverse = 10000.0 ** (-jnp.arange(0, ROT, 2).astype(jnp.float32) / ROT)
    phases = places.astype(jnp.float32)[:, None] * inverse[None, :]
    return (jnp.cos(phases), jnp.sin(phases))


def rotate(values, cosine, sine):
    half_rot = cosine.shape[-1]
    front = values[..., :half_rot]
    second = values[..., half_rot : 2 * half_rot]
    others = values[..., 2 * half_rot :]
    cos_b = cosine[:, None, :]
    sin_b = sine[:, None, :]
    return jnp.concatenate(
        [front * cos_b - second * sin_b, second * cos_b + front * sin_b, others], axis=-1
    )


def adam_step(weight, gradient, moment, second, rate, decay):
    moment = 0.9 * moment + 0.1 * gradient
    second = 0.95 * second + 0.05 * gradient * gradient
    unbiased = moment / (1.0 - 0.9**STEP)
    scaled = second / (1.0 - 0.95**STEP)
    return (weight - rate * (unbiased / (jnp.sqrt(scaled) + 1e-08) + decay * weight), second)


def general_device(
    layer_input,
    out_grad,
    positions,
    w_qkv,
    w_dense,
    w_up,
    w_down,
    vectors,
    m_qkv,
    m_dense,
    m_up,
    m_down,
    m_vectors,
    v_qkv,
    v_dense,
    v_up,
    v_down,
    v_vectors,
):
    block_rows = layer_input.shape[1]
    model_width = layer_input.shape[2]
    hidden = w_up.shape[1]
    rows_in = w_qkv.shape[0]
    rows_down = w_down.shape[0]
    n_ctx = lax.axis_size("ctx")
    score_scale = HD ** (-0.5)
    ctx_index = lax.axis_index("ctx")
    all_pos = positions[0]
    own_pos = lax.dynamic_slice_in_dim(all_pos, ctx_index * block_rows, block_rows)
    last_own = jnp.max(own_pos)
    cosine, sine = angles(own_pos)
    full_vec = lax.all_gather(vectors, ("ctx", "shard"), axis=1, tiled=True)
    tokens = layer_input[0].astype(jnp.float32)
    normed_one = layer_norm(tokens, full_vec[0], full_vec[1]).astype(jnp.bfloat16)
    normed_two = layer_norm(tokens, full_vec[2], full_vec[3]).astype(jnp.bfloat16)
    qkv_low = w_qkv.astype(jnp.bfloat16)
    dense_low = w_dense.astype(jnp.bfloat16)
    up_low = w_up.astype(jnp.bfloat16)
    down_low = w_down.astype(jnp.bfloat16)
    grad_low = out_grad[0]
    grad_rows = grad_low.astype(jnp.float32)
    pieces = (
        lax.all_gather(qkv_low, ("ctx", "shard"), axis=0, tiled=True),
        lax.all_gather(up_low, ("ctx", "shard"), axis=0, tiled=True),
    )
    left_one = normed_one
    left_two = normed_two
    proj_sum = jnp.dot(left_one, pieces[0], preferred_element_type=jnp.float32)
    up_sum = jnp.dot(left_two, pieces[1], preferred_element_type=jnp.float32)
    projection = proj_sum + full_vec[4:7].reshape(-1)
    up_value = up_sum + full_vec[8:12].reshape(-1)
    queries = projection[:, :model_width].reshape(block_rows, H, HD)
    keys_raw = projection[:, model_width : 2 * model_width].reshape(block_rows, H, HD)
    values_raw = projection[:, 2 * model_width :].reshape(block_rows, H, HD)
    q_rot = rotate(queries, cosine, sine).astype(jnp.bfloat16)
    k_rot = rotate(keys_raw, cosine, sine).astype(jnp.bfloat16)
    v_low = values_raw.astype(jnp.bfloat16)
    start_state = (
        jnp.full((block_rows, H), -1e30, jnp.float32),
        jnp.zeros((block_rows, H), jnp.float32),
        jnp.zeros((block_rows, H, HD), jnp.float32),
    )
    pieces = (
        lax.all_gather(k_rot, "ctx", axis=0, tiled=True),
        lax.all_gather(v_low, "ctx", axis=0, tiled=True),
    )
    key_pos = all_pos
    allowed = (key_pos[None, :] <= own_pos[:, None])[:, None, :]

    def attend_compute(states):
        running_top, totals, accum = states
        scores = (
            jnp.einsum("qhd,khd->qhk", q_rot, pieces[0], preferred_element_type=jnp.float32)
            * score_scale
        )
        scores = jnp.where(allowed, scores, -1e30)
        new_top = jnp.maximum(running_top, jnp.max(scores, axis=-1))
        weights = jnp.where(allowed, jnp.exp(scores - new_top[..., None]), 0.0)
        totals = jnp.sum(weights, axis=-1)
        accum = jnp.einsum(
            "qhk,khd->qhd",
            weights.astype(jnp.bfloat16),
            pieces[1],
            preferred_element_type=jnp.float32,
        )
        return (new_top, totals, accum)

    skipped = jnp.min(key_pos) > last_own
    running_top, totals, accum = lax.cond(
        skipped, lambda states: states, attend_compute, start_state
    )
    attention = accum / totals[..., None]
    log_sum = running_top + jnp.log(totals)
    attn_low = attention.reshape(block_rows, model_width).astype(jnp.bfloat16)
    gelu_exact = partial(jax.nn.gelu, approximate=False)
    hid_low = gelu_exact(up_value).astype(jnp.bfloat16)
    add_pieces = (
        lax.all_gather(dense_low, ("ctx", "shard"), axis=0, tiled=True),
        lax.all_gather(down_low, ("ctx", "shard"), axis=0, tiled=True),
    )
    second_count = add_pieces[1].shape[0]
    second_begin = jnp.int32(0) // rows_in * rows_down
    left_attn = attn_low
    left_hid = lax.dynamic_slice_in_dim(hid_low, second_begin, second_count, 1)
    branches = jnp.dot(left_attn, add_pieces[0], preferred_element_type=jnp.float32) + jnp.dot(
        left_hid, add_pieces[1], preferred_element_type=jnp.float32
    )
    back_pieces = lax.all_gather((dense_low, down_low), ("ctx", "shard"), axis=0, tiled=True)
    shard_count = back_pieces[0].shape[0] // rows_in
    first_part = jnp.einsum(
        "td,rd->tr", grad_low, back_pieces[0], preferred_element_type=jnp.float32
    ).reshape(block_rows, shard_count, rows_in)
    second_part = jnp.einsum(
        "td,rd->tr", grad_low, back_pieces[1], preferred_element_type=jnp.float32
    ).reshape(block_rows, shard_count, rows_down)
    merged_out = jnp.concatenate([first_part, second_part], axis=2).reshape(
        block_rows, shard_count * (rows_in + rows_down)
    )
    merged_out = merged_out.reshape(block_rows, -1, rows_in + rows_down)
    grad_attn = merged_out[:, :, :rows_in].reshape(block_rows, model_width)
    grad_hid = merged_out[:, :, rows_in:].reshape(block_rows, hidden)
    layer_output = (tokens + branches + full_vec[7] + full_vec[12]).astype(jnp.bfloat16)[None]
    gelu_pull = jax.vjp(gelu_exact, up_value)[1]
    grad_upval = gelu_pull(grad_hid)[0].astype(jnp.bfloat16)
    grad_heads = grad_attn.astype(jnp.bfloat16).reshape(block_rows, H, HD)
    delta_rows = jnp.sum(grad_heads.astype(jnp.float32) * attention, axis=-1)

    def key_turn(turn_index, states):
        pair_now, pair_grad, query_grad = states
        owner_index = (ctx_index - turn_index) % n_ctx
        key_pos = lax.dynamic_slice_in_dim(all_pos, owner_index * block_rows, block_rows)
        allowed = (key_pos[None, :] <= own_pos[:, None])[:, None, :]

        def key_compute(partials):
            grads_held, query_held = partials
            scores = (
                jnp.einsum("qhd,khd->qhk", q_rot, pair_now[0], preferred_element_type=jnp.float32)
                * score_scale
            )
            weights_now = jnp.where(allowed, jnp.exp(scores - log_sum[..., None]), 0.0)
            grad_prob = jnp.einsum(
                "qhd,khd->qhk", grad_heads, pair_now[1], preferred_element_type=jnp.float32
            )
            dscore = (weights_now * (grad_prob - delta_rows[..., None])).astype(jnp.bfloat16)
            query_held = (
                query_held
                + jnp.einsum(
                    "qhk,khd->qhd", dscore, pair_now[0], preferred_element_type=jnp.float32
                )
                * score_scale
            )
            key_term = (
                jnp.einsum("qhk,qhd->khd", dscore, q_rot, preferred_element_type=jnp.float32)
                * score_scale
            )
            value_term = jnp.einsum(
                "qhk,qhd->khd",
                weights_now.astype(jnp.bfloat16),
                grad_heads,
                preferred_element_type=jnp.float32,
            )
            return (grads_held + jnp.stack([key_term, value_term]), query_held)

        skipped = jnp.min(key_pos) > last_own
        pair_grad, query_grad = lax.cond(
            skipped, lambda partials: partials, key_compute, (pair_grad, query_grad)
        )
        pair_now = from_behind(pair_now, "ctx", 1)
        pair_grad = from_behind(pair_grad.astype(jnp.bfloat16), "ctx", 1).astype(pair_grad.dtype)
        return (pair_now, pair_grad, query_grad)

    loop_start = (
        jnp.stack([k_rot, v_low]),
        jnp.zeros((2, block_rows, H, HD), jnp.float32),
        jnp.zeros((block_rows, H, HD), jnp.float32),
    )
    loop_end = lax.fori_loop(0, n_ctx, key_turn, loop_start)
    pair_grad = loop_end[1]
    query_grad = loop_end[2]

    def turn_values(values):
        return rotate(values, cosine, sine)

    rot_pull = jax.vjp(turn_values, queries)[1]
    grad_proj = jnp.concatenate(
        [
            rot_pull(query_grad)[0].reshape(block_rows, model_width),
            rot_pull(pair_grad[0])[0].reshape(block_rows, model_width),
            pair_grad[1].reshape(block_rows, model_width),
        ],
        axis=1,
    ).astype(jnp.bfloat16)

    def back_inputs(pieces):
        shard_count = pieces[0].shape[0] // rows_in
        first_part = jnp.einsum(
            "tc,rc->tr", grad_proj, pieces[0], preferred_element_type=jnp.float32
        ).reshape(block_rows, shard_count, 1, rows_in)
        second_part = jnp.einsum(
            "tc,rc->tr", grad_upval, pieces[1], preferred_element_type=jnp.float32
        ).reshape(block_rows, shard_count, 1, rows_in)
        return jnp.concatenate([first_part, second_part], axis=2).reshape(
            block_rows, shard_count * 2 * rows_in
        )

    merged_in = back_inputs(lax.all_gather((qkv_low, up_low), ("ctx", "shard"), axis=0, tiled=True))
    merged_in = merged_in.reshape(block_rows, -1, 2, rows_in)
    grad_norm_one = merged_in[:, :, 0].reshape(block_rows, model_width)
    grad_norm_two = merged_in[:, :, 1].reshape(block_rows, model_width)
    norm_pull_one = jax.vjp(layer_norm, tokens, full_vec[0], full_vec[1])[1]
    norm_pull_two = jax.vjp(layer_norm, tokens, full_vec[2], full_vec[3])[1]
    back_one, gain_one, shift_one = norm_pull_one(grad_norm_one)
    back_two, gain_two, shift_two = norm_pull_two(grad_norm_two)
    grad_input = (grad_rows + back_one + back_two)[None]
    column_out = jnp.sum(grad_rows, axis=0)
    vector_terms = jnp.concatenate(
        [
            jnp.stack([gain_one, shift_one, gain_two, shift_two]),
            jnp.sum(grad_proj.astype(jnp.float32), axis=0).reshape(3, model_width),
            column_out[None],
            jnp.sum(grad_upval.astype(jnp.float32), axis=0).reshape(4, model_width),
            column_out[None],
        ],
        axis=0,
    )
    grad_vectors = lax.psum_scatter(vector_terms, ("ctx", "shard"), scatter_dimension=1, tiled=True)
    block_count = (rows_in + rows_down) * lax.axis_size(("ctx", "shard")) // (rows_in + rows_down)
    first_block = jnp.int32(0) // (rows_in + rows_down)
    left_attn = attn_low
    left_hid = lax.dynamic_slice_in_dim(
        hid_low, first_block * rows_down, block_count * rows_down, 1
    )
    dense_part = jnp.einsum(
        "tr,td->rd", left_attn, grad_low, preferred_element_type=jnp.float32
    ).reshape(block_count, rows_in, model_width)
    down_part = jnp.einsum(
        "tr,td->rd", left_hid, grad_low, preferred_element_type=jnp.float32
    ).reshape(block_count, rows_down, model_width)
    out_grads = lax.psum_scatter(
        jnp.concatenate([dense_part, down_part], axis=1).reshape(
            (rows_in + rows_down) * lax.axis_size(("ctx", "shard")), model_width
        ),
        ("ctx", "shard"),
        scatter_dimension=0,
        tiled=True,
    )
    left_one = normed_one
    left_two = normed_two
    in_grads = lax.psum_scatter(
        jnp.concatenate(
            [
                jnp.einsum("tr,tc->rc", left_one, grad_proj, preferred_element_type=jnp.float32),
                jnp.einsum("tr,tc->rc", left_two, grad_upval, preferred_element_type=jnp.float32),
            ],
            axis=1,
        ),
        ("ctx", "shard"),
        scatter_dimension=0,
        tiled=True,
    )
    grad_qkv = in_grads[:, : 3 * model_width]
    grad_up = in_grads[:, 3 * model_width :]
    grad_dense = out_grads[:rows_in]
    grad_down = out_grads[rows_in:]
    new_qkv, second_qkv = adam_step(w_qkv, grad_qkv, m_qkv, v_qkv, 4.0 * (D // 2) ** (-0.5), 0.1)
    new_dense, second_dense = adam_step(
        w_dense, grad_dense, m_dense, v_dense, 4.0 * (D // 32) ** (-0.5), 0.1
    )
    new_up, second_up = adam_step(w_up, grad_up, m_up, v_up, 4.0 * D ** (-0.5), 0.1)
    new_down, second_down = adam_step(w_down, grad_down, m_down, v_down, 4.0 * FF ** (-0.5), 0.1)
    new_vectors, second_vectors = adam_step(vectors, grad_vectors, m_vectors, v_vectors, 1.0, 0.0)
    return (
        layer_output,
        grad_input,
        grad_qkv,
        grad_dense,
        grad_up,
        grad_down,
        grad_vectors,
        second_qkv,
        second_dense,
        second_up,
        second_down,
        second_vectors,
        new_qkv,
        new_dense,
        new_up,
        new_down,
        new_vectors,
    )


MESH = pl.DeviceIdType.MESH
VMEM_BYTES = 62 * 1024 * 1024


def push(source, target, sent, arrived, **device):
    return pltpu.make_async_remote_copy(
        src_ref=source,
        dst_ref=target,
        send_sem=sent,
        recv_sem=arrived,
        device_id=device,
        device_id_type=MESH,
    )


class Spot:
    def __init__(self, n_plane, n_shard):
        self.n_plane, self.n_shard = n_plane, n_shard
        self.plane = lax.axis_index("plane")
        self.core = lax.axis_index("core")
        self.shard = lax.axis_index("shard")
        self.slot = self.core * n_shard + self.shard
        head = 2 * self.plane + self.core
        self.head_core = lax.div(head, n_shard)
        self.head_shard = lax.rem(head, n_shard)
        self.owner_plane = lax.div(self.slot, 2)
        self.owner_core = lax.rem(self.slot, 2)
        self.head_here = jnp.logical_and(self.slot == head, self.plane == self.shard)

    def group(self):
        for turn in range(1, 2 * self.n_shard):
            yield turn - 1, self.turned(turn)

    def turned(self, turn):
        core = lax.rem(self.core + turn // self.n_shard, 2)
        shard = lax.rem(self.shard + turn % self.n_shard, self.n_shard)
        return dict(core=core, shard=shard)

    def beside(self):
        across = self.plane + 1 - 2 * lax.rem(self.plane, 2)
        return across, lax.rem(self.plane + 2, 4), 3 - self.plane

    def along(self):
        for step in range(1, self.n_shard):
            yield step - 1, lax.rem(self.shard + step, self.n_shard)

    def planes(self):
        for step in range(1, self.n_plane):
            yield step - 1, lax.rem(self.plane + step, self.n_plane)

    def keeper(self):
        return dict(plane=self.shard, core=self.head_core, shard=self.head_shard)

    def owner(self):
        return dict(plane=self.owner_plane, core=self.owner_core, shard=self.plane)

    def greet(self, sender):
        barrier = pltpu.get_barrier_semaphore()
        count = 0
        for _, device in self.group():
            pl.semaphore_signal(barrier, inc=1, device_id=device, device_id_type=MESH)
            count += 1
        for _, plane in self.planes():
            pl.semaphore_signal(barrier, inc=1, device_id=dict(plane=plane), device_id_type=MESH)
            count += 1

        @pl.when(jnp.logical_not(self.head_here))
        def _():
            pl.semaphore_signal(barrier, inc=1, device_id=sender, device_id_type=MESH)
            pl.semaphore_wait(barrier, count + 1)

        @pl.when(self.head_here)
        def _():
            pl.semaphore_wait(barrier, count)


def turn_tables(pos_row, freq):
    n_pos = pos_row.shape[1]
    places = jnp.broadcast_to(pos_row.astype(jnp.float32), (n_pos, n_pos)).T
    phase = places * freq
    return jnp.cos(phase), jnp.sin(phase), places


def turn(head, cosine, sine):
    half = ROT // 2
    lanes = cosine.shape[1]
    front = head[:, :lanes]
    lane = lax.broadcasted_iota(jnp.int32, front.shape, 1)
    first = jnp.where(lane < half, -sine, 0.0)
    second = jnp.where((lane >= half) & (lane < ROT), sine, 0.0)
    turned = (
        front * cosine
        + pltpu.roll(front, lanes - half, 1) * first
        + pltpu.roll(front, half, 1) * second
    )
    return jnp.concatenate([turned, head[:, lanes:]], axis=1)


def dot(left, right, left_dim=1, right_dim=0):
    return lax.dot_general(
        left, right, (((left_dim,), (right_dim,)), ((), ())), preferred_element_type=jnp.float32
    )


class Spread:
    def __init__(self, spot, ref, size, sent, here):
        self.spot, self.ref, self.size, self.sent, self.here = spot, ref, size, sent, here
        self.across, self.along, self.diagonal = spot.beside()

    def rows(self, plane, part=None):
        size = self.size
        if part is None:
            return self.ref.at[pl.ds(pl.multiple_of(plane * size, size), size)]
        half = size // 2
        return self.ref.at[pl.ds(pl.multiple_of(plane * size + part * half, half), half)]

    def send(self, rows, place, plane):
        return push(rows, rows, self.sent.at[place], self.here.at[place], plane=plane)

    def first(self):
        own = self.rows(self.spot.plane)
        return [self.send(own, 0, self.across), self.send(own, 1, self.along)]

    def second(self):
        return [
            self.send(self.rows(self.along, 0), 2, self.across),
            self.send(self.rows(self.across, 1), 3, self.along),
        ]

    def start(self):
        for copy in self.first():
            copy.start()

    def relay(self):
        first, second = self.first(), self.second()
        first[1].wait_recv()
        second[0].start()
        first[0].wait_recv()
        second[1].start()

    def finish(self):
        for copy in self.second():
            copy.wait_recv()

    def finish_sends(self):
        for copy in self.first() + self.second():
            copy.wait_send()


class Gather:
    def __init__(self, spot, part, size, landed, sent, here):
        self.spot, self.part, self.size, self.landed = spot, part, size, landed
        self.sent, self.here = sent, here
        self.across, self.along, self.diagonal = spot.beside()

    def rows(self, plane, side):
        half = self.size // 2
        return self.part.at[pl.ds(pl.multiple_of(plane * self.size + side * half, half), half)]

    def send(self, rows, place, plane):
        return push(
            rows, self.landed.at[place], self.sent.at[place], self.here.at[place], plane=plane
        )

    def first(self):
        return [
            self.send(self.rows(self.diagonal, 0), 0, self.across),
            self.send(self.rows(self.diagonal, 1), 1, self.along),
            self.send(self.rows(self.across, 0), 2, self.across),
            self.send(self.rows(self.along, 1), 3, self.along),
        ]

    def second(self):
        return [
            self.send(self.rows(self.along, 0), 4, self.along),
            self.send(self.rows(self.across, 1), 5, self.across),
        ]

    def start(self):
        for copy in self.first():
            copy.start()

    def relay(self):
        first, second = self.first(), self.second()
        for side in range(2):
            first[side].wait_recv()
            held = self.rows(self.along if side == 0 else self.across, side)
            add_rows(held, [held, self.landed.at[side]], self.size // 2)
            second[side].start()

    def own(self):
        size = self.size
        return self.part.at[pl.ds(pl.multiple_of(self.spot.plane * size, size), size)]

    def finish(self):
        first, second = self.first(), self.second()
        half = self.size // 2
        for side in range(2):
            first[2 + side].wait_recv()
            second[side].wait_recv()
            held = self.rows(self.spot.plane, side)
            add_rows(held, [held, self.landed.at[2 + side], self.landed.at[4 + side]], half)

    def finish_sends(self):
        for copy in self.first() + self.second():
            copy.wait_send()


class RowSum:
    def __init__(self, spot, part, landed, sent, here):
        self.spot, self.part, self.landed = spot, part, landed
        self.sent, self.here = sent, here

    def rows(self, shard):
        return self.part.at[shard]

    def place(self, side, at, shard):
        if side == 0:
            return shard
        return jnp.where(shard == at, self.spot.n_shard, shard)

    def hop(self, side, shard):
        spot = self.spot
        to = spot.shard + (1 if side == 0 else -1)
        return push(
            self.rows(shard),
            self.landed.at[self.place(side, to, shard)],
            self.sent.at[side, shard],
            self.here.at[side, shard],
            shard=to,
        )

    def wait(self, side, shard):
        spot = self.spot
        push(
            self.rows(shard),
            self.landed.at[self.place(side, spot.shard, shard)],
            self.sent.at[side, shard],
            self.here.at[side, shard],
            shard=spot.shard,
        ).wait_recv()

    def start(self):
        spot, last = self.spot, self.spot.n_shard - 1
        for side in range(2):

            @pl.when(spot.shard == (0 if side == 0 else last))
            def _():
                for step in range(last):
                    self.hop(side, last - step if side == 0 else step).start()

    def relay(self, turn):
        spot, last = self.spot, self.spot.n_shard - 1
        for side in range(2):
            depth = spot.shard if side == 0 else last - spot.shard
            shard = last - turn + spot.shard if side == 0 else turn - last + spot.shard

            @pl.when(jnp.logical_and(depth >= 1, depth <= turn))
            def _():
                self.wait(side, shard)
                held = self.rows(shard)
                came = self.landed.at[self.place(side, spot.shard, shard)]
                add_rows(held, [held, came], held.shape[0])
                self.hop(side, shard).start()

    def finish(self, target):
        spot, last = self.spot, self.spot.n_shard - 1
        held = self.rows(spot.shard)
        first = self.landed.at[self.place(0, spot.shard, spot.shard)]
        second = self.landed.at[self.place(1, spot.shard, spot.shard)]

        @pl.when(spot.shard >= 1)
        def _():
            self.wait(0, spot.shard)

        @pl.when(spot.shard < last)
        def _():
            self.wait(1, spot.shard)

        @pl.when(spot.shard == 0)
        def _():
            add_rows(target, [held, second], held.shape[0])

        @pl.when(spot.shard == last)
        def _():
            add_rows(target, [held, first], held.shape[0])

        @pl.when(jnp.logical_and(spot.shard >= 1, spot.shard < last))
        def _():
            add_rows(target, [held, first, second], held.shape[0])

    def finish_sends(self):
        spot = self.spot
        for shard in range(spot.n_shard):
            for side in range(2):

                @pl.when(spot.shard < shard if side == 0 else spot.shard > shard)
                def _():
                    self.hop(side, shard).wait_send()


class Chain:
    def __init__(self, spot, ref, block, sent, here, pair_sent, pair_here):
        self.spot, self.ref, self.block = spot, ref, block
        self.sent, self.here = sent, here
        self.pair_sent, self.pair_here = pair_sent, pair_here

    def rows(self, shard, core):
        start = pl.multiple_of((shard * 2 + core) * self.block, self.block)
        return self.ref.at[pl.ds(start, self.block)]

    def hop(self, side, dist):
        spot = self.spot
        sign = 1 if side == 0 else -1
        rows = self.rows(spot.shard - sign * dist, spot.core)
        return push(
            rows, rows, self.sent.at[side, dist], self.here.at[side, dist], shard=spot.shard + sign
        )

    def pair(self, side, dist):
        spot = self.spot
        sign = 1 if side == 0 else -1
        rows = self.rows(spot.shard - sign * dist, spot.core)
        return push(
            rows,
            rows,
            self.pair_sent.at[side, dist],
            self.pair_here.at[side, dist],
            core=1 - spot.core,
        )

    def holds(self, side, dist):
        spot = self.spot
        return spot.shard >= dist if side == 0 else spot.shard + dist < spot.n_shard

    def goes(self, side, dist):
        spot = self.spot
        more = spot.shard + 1 < spot.n_shard if side == 0 else spot.shard >= 1
        return jnp.logical_and(self.holds(side, dist), more)

    def start(self):
        for side in range(2):

            @pl.when(self.goes(side, 0))
            def _():
                self.hop(side, 0).start()

        self.pair(0, 0).start()

    def step(self, dist):
        for side in range(2):

            @pl.when(self.holds(side, dist))
            def _():
                self.hop(side, dist - 1).wait_recv()
                if dist + 1 < self.spot.n_shard:

                    @pl.when(self.goes(side, dist))
                    def _():
                        self.hop(side, dist).start()

                self.pair(side, dist).start()

    def finish_pairs(self):
        self.pair(0, 0).wait_recv()
        for dist in range(1, self.spot.n_shard):
            for side in range(2):

                @pl.when(self.holds(side, dist))
                def _():
                    self.pair(side, dist).wait_recv()

    def finish_sends(self):
        self.pair(0, 0).wait_send()
        for side in range(2):
            for dist in range(self.spot.n_shard - 1):

                @pl.when(self.goes(side, dist))
                def _():
                    self.hop(side, dist).wait_send()

            for dist in range(1, self.spot.n_shard):

                @pl.when(self.holds(side, dist))
                def _():
                    self.pair(side, dist).wait_send()


def forward_kernel(
    n_plane,
    n_shard,
    x_ref,
    dy_ref,
    pos_ref,
    vec_ref,
    freq_ref,
    wq_ref,
    wu_ref,
    wd_ref,
    wo_ref,
    x_out,
    dy_out,
    one_out,
    two_out,
    hid_out,
    gup_out,
    back_out,
    wq_out,
    wu_out,
    wd_out,
    wo_out,
    vec_out,
    moments_out,
    x_all,
    dy_all,
    one,
    two,
    wq_all,
    wu_all,
    wd_all,
    wo_all,
    vec_all,
    pos_all,
    full_vec,
    wu_raw,
    wd_raw,
    wo_raw,
    wq_cut,
    wu_cut,
    wo_cut,
    to_heads,
    heads,
    from_heads,
    back,
    grad_k,
    grad_v,
    cos_head,
    sin_head,
    place_head,
    cos_row,
    sin_row,
    key_row,
    probs,
    slope,
    attention,
    moments,
    loads,
    stores,
    local,
    x_sent,
    x_here,
    x_pair_sent,
    x_pair_here,
    dy_sent,
    dy_here,
    dy_pair_sent,
    dy_pair_here,
    pos_sent,
    pos_here,
    cols_sent,
    cols_here,
    flat_sent,
    flat_here,
    spread_sent,
    spread_here,
    swap_sent,
    swap_here,
    head_sent,
    head_here,
):
    spot = Spot(n_plane, n_shard)
    plane, core, shard, slot = spot.plane, spot.core, spot.shard, spot.slot
    f32, bf16 = jnp.float32, jnp.bfloat16
    block = x_ref.shape[0]
    pair = 2 * block
    n_slice = 2 * n_shard
    rows_in, rows_down = wq_ref.shape[0], wd_ref.shape[0]
    width = x_ref.shape[1]
    n_group = n_slice * block

    def piece(ref, at, size):
        return ref.at[pl.ds(pl.multiple_of(at * size, size), size)]

    chain_x = Chain(spot, x_all, block, x_sent, x_here, x_pair_sent, x_pair_here)
    chain_dy = Chain(spot, dy_all, block, dy_sent, dy_here, dy_pair_sent, dy_pair_here)

    raw = [
        pltpu.make_async_copy(source, held, loads.at[place])
        for place, (source, held) in enumerate(
            [
                (wq_ref, wu_raw.at[:, pl.ds(0, wq_ref.shape[1])]),
                (wu_ref, wu_raw),
                (wd_ref, wd_raw),
                (wo_ref, wo_raw),
                (x_ref, chain_x.rows(shard, core)),
                (dy_ref, chain_dy.rows(shard, core)),
                (pos_ref, pos_all.at[shard]),
                (vec_ref, vec_all.at[plane, slot]),
            ]
        )
    ]
    for place, copy in enumerate(raw):
        if place != 1:
            copy.start()
    spot.greet(spot.owner())

    index = plane * n_slice + slot
    wq_own = piece(wq_all, index, rows_in)
    wu_own = piece(wu_all, index, rows_in)

    def to_group(place, source, target):
        return [
            push(
                source(device["core"] * n_shard + device["shard"]),
                target,
                cols_sent.at[place, turn_at],
                cols_here.at[place, turn_at],
                **device,
            )
            for turn_at, device in spot.group()
        ]

    cols_q = to_group(0, lambda to: wq_cut.at[to], wq_own)
    cols_u = to_group(1, lambda to: wu_cut.at[to], wu_own)
    cols_v = to_group(2, lambda to: vec_all.at[plane, slot], vec_all.at[plane, slot])

    def to_planes(place, ref):
        return [
            push(ref, ref, flat_sent.at[place, turn_at], flat_here.at[place, turn_at], plane=to)
            for turn_at, to in spot.planes()
        ]

    group_rows = n_slice * rows_in
    spread_d = Spread(spot, wd_all, rows_down, spread_sent.at[0], spread_here.at[0])
    spread_q = Spread(spot, wq_all, group_rows, spread_sent.at[1], spread_here.at[1])
    spread_u = Spread(spot, wu_all, group_rows, spread_sent.at[2], spread_here.at[2])
    flat_v = to_planes(0, vec_all.at[plane])
    flat_o = to_planes(1, piece(wo_all, plane, rows_in))
    pos_push = [
        push(
            pos_all.at[shard],
            pos_all.at[shard],
            pos_sent.at[turn_at],
            pos_here.at[turn_at],
            shard=to,
        )
        for turn_at, to in spot.along()
    ]

    raw[6].wait()
    raw[7].wait()
    for copy in cols_v + pos_push:
        copy.start()

    raw[4].wait()
    chain_x.start()
    raw[0].wait()
    for to in range(n_slice):
        for part in range(3):
            wq_cut[to, :, part * HD : (part + 1) * HD] = wu_raw[
                :, part * width + to * HD : part * width + (to + 1) * HD
            ].astype(bf16)
    raw[1].start()
    for copy in cols_q:
        copy.start()
    keep_q = pltpu.make_async_copy(wq_cut.at[slot], wq_own, local.at[0])
    keep_q.start()
    for copy in cols_v:
        copy.wait_recv()
    for copy in flat_v:
        copy.start()
    raw[2].wait()

    down_at = plane * rows_down

    @pl.loop(0, rows_down // 32)
    def _(step):
        at = pl.multiple_of(step * 32, 32)
        wd_all[pl.ds(pl.multiple_of(down_at + at, 32), 32), :] = wd_raw[pl.ds(at, 32), :].astype(bf16)

    spread_d.start()
    raw[1].wait()
    for to in range(n_slice):
        for part in range(n_plane):
            wu_cut[to, :, part * rows_down : (part + 1) * rows_down] = wu_raw[
                :, part * width + to * rows_down : part * width + (to + 1) * rows_down
            ].astype(bf16)
    keep_u = pltpu.make_async_copy(wu_cut.at[slot], wu_own, local.at[1])
    keep_u.start()
    raw[3].wait()
    wo_cut[...] = wo_raw[...].astype(bf16)
    head_rows = piece(wo_all, shard, rows_in)
    to_head = push(wo_cut, head_rows, head_sent, head_here, **spot.keeper())
    own_head = pltpu.make_async_copy(wo_cut, head_rows, head_sent)

    @pl.when(spot.head_here)
    def _():
        own_head.start()

    @pl.when(jnp.logical_not(spot.head_here))
    def _():
        to_head.start()

    raw[5].wait()
    chain_x.step(1)
    for copy in cols_u:
        copy.start()
    spread_d.relay()
    chain_dy.start()
    keep_q.wait()
    for copy in cols_q:
        copy.wait_recv()
    spread_q.start()
    chain_x.step(2)

    for copy in pos_push:
        copy.wait_recv()
    freq = freq_ref[...]
    own_blocks = 2 * plane

    @pl.loop(0, n_shard)
    def _(seq):
        for half in range(2):
            at = pl.ds(pl.multiple_of(seq * pair + half * block, block), block)
            cosine, sine, _ = turn_tables(pos_all[seq, pl.ds(own_blocks + half, 1), :], freq)
            cos_row[at, :] = cosine
            sin_row[at, :] = sine

    spread_q.relay()
    keep_u.wait()
    for copy in cols_u:
        copy.wait_recv()
    spread_u.start()
    chain_dy.step(1)
    for dist in range(3, n_shard):
        chain_x.step(dist)

    @pl.when(spot.head_here)
    def _():
        own_head.wait()

    @pl.when(jnp.logical_not(spot.head_here))
    def _():
        to_head.wait_recv()

    for copy in flat_o:
        copy.start()

    @pl.loop(0, n_plane)
    def _(part):
        for half in range(2):
            at = pl.ds(pl.multiple_of(part * pair + half * block, block), block)
            cosine, sine, places = turn_tables(pos_all[plane, pl.ds(2 * part + half, 1), :], freq)
            cos_head[at, :] = cosine
            sin_head[at, :] = sine
            place_head[at, :] = places

    for at in range(pos_all.shape[1]):
        key_row[:, at * block : (at + 1) * block] = pos_all[plane, pl.ds(at, 1), :].astype(f32)

    for copy in flat_v:
        copy.wait_recv()
    n_vec, lanes = vec_all.shape[2:]
    lane = lax.broadcasted_iota(jnp.int32, (n_vec, lanes), 1)
    for p in range(n_plane):
        for t in range(0, n_slice, 2):
            at = (p * n_slice + t) * (lanes // 2)
            full_vec[:, at : at + lanes] = jnp.where(
                lane < lanes // 2, vec_all[p, t], pltpu.roll(vec_all[p, t + 1], lanes // 2, 1)
            )
    save_vec = pltpu.make_async_copy(full_vec, vec_out, stores.at[0])
    save_vec.start()

    chain_x.finish_pairs()
    save_x = pltpu.make_async_copy(x_all, x_out, stores.at[1])
    save_x.start()

    def norm_rows(seq):
        @pl.loop(0, pair // 32)
        def _(step):
            at = pl.ds(pl.multiple_of(seq * pair + step * 32, 32), 32)
            tokens = x_all[at, :].astype(f32)
            mean = jnp.mean(tokens, axis=-1, keepdims=True)
            center = tokens - mean
            scale = lax.rsqrt(jnp.mean(center * center, axis=-1, keepdims=True) + 1e-05)
            lane = lax.broadcasted_iota(jnp.int32, (32, moments.shape[1]), 1)
            moments[at, :] = jnp.where(lane < 1, mean, scale)
            hat = center * scale
            one[at, :] = (hat * full_vec[0:1, :] + full_vec[1:2, :]).astype(bf16)
            two[at, :] = (hat * full_vec[2:3, :] + full_vec[3:4, :]).astype(bf16)

    for seq in range(n_shard):
        norm_rows(seq)
        if seq == 1:
            chain_dy.step(2)
            spread_u.relay()
    save_moments = pltpu.make_async_copy(moments, moments_out, stores.at[12])
    save_moments.start()
    save_one = pltpu.make_async_copy(one, one_out, stores.at[2])
    save_one.start()
    save_two = pltpu.make_async_copy(two, two_out, stores.at[3])
    save_two.start()

    spread_q.finish()
    save_wq = pltpu.make_async_copy(wq_all, wq_out, stores.at[4])
    save_wq.start()
    head_lanes = pl.ds(pl.multiple_of(slot * HD, HD), HD)

    def swap(place, source, target, cols, to, turn_at):
        def piece_of(ref, at):
            return ref.at[pl.ds(pl.multiple_of(at * pair, pair), pair), cols]

        return push(
            piece_of(source, to),
            piece_of(target, plane),
            swap_sent.at[place, turn_at - 1],
            swap_here.at[place, turn_at - 1],
            plane=to,
        )

    def keep_own(place, source, target, cols):
        at = pl.ds(pl.multiple_of(plane * pair, pair), pair)
        return pltpu.make_async_copy(source.at[at, cols], target.at[at, cols], local.at[place])

    def swaps(place, source, target, cols):
        return [
            swap(place, source, target, cols, lax.rem(plane + turn_at, n_plane), turn_at)
            for turn_at in range(1, n_plane)
        ]

    qkv_cols = pl.ds(0, 3 * HD)
    q_cols, kv_cols, o_cols = pl.ds(0, HD), pl.ds(HD, 2 * HD), pl.ds(3 * HD, HD)

    for step in range(2):
        at = slice(step * 2 * pair, (step + 1) * 2 * pair)
        heads_now = dot(one[at, :], wq_all[...])
        for part in range(3):
            cols = slice(part * HD, (part + 1) * HD)
            value = heads_now[:, cols] + full_vec[4 + part : 5 + part, head_lanes]
            if part < 2:
                value = turn(value, cos_row[at, :], sin_row[at, :])
            to_heads[at, cols] = value.astype(bf16)

    for copy in swaps(0, to_heads, heads, qkv_cols):
        copy.start()
    keep_qkv = keep_own(2, to_heads, heads, qkv_cols)
    keep_qkv.start()

    spread_u.finish()
    save_wu = pltpu.make_async_copy(wu_all, wu_out, stores.at[8])
    save_wu.start()
    save_one.wait()
    up_lanes = pl.ds(pl.multiple_of(slot * rows_down, rows_down), rows_down)
    n_hid = n_plane * rows_down

    def hidden_rows(step):
        at = pl.ds(pl.multiple_of(step * pair, pair), pair)
        hidden = dot(two[at, :], wu_all[...])
        for part in range(n_plane):
            cols = slice(part * rows_down, (part + 1) * rows_down)
            value = hidden[:, cols] + full_vec[8 + part : 9 + part, up_lanes]
            half = 0.5 + 0.5 * lax.erf(value * 0.7071067811865476)
            slope[at, cols] = half + value * (0.3989422804014327 * jnp.exp(-0.5 * value * value))
            one[at, cols] = (value * half).astype(bf16)

    @pl.loop(0, n_shard)
    def _(step):
        hidden_rows(step)

    for dist in range(3, n_shard):
        chain_dy.step(dist)

    save_hid = pltpu.make_async_copy(one.at[:, 0:n_hid], hid_out, stores.at[9])
    save_hid.start()

    chain_dy.finish_pairs()
    save_dy = pltpu.make_async_copy(dy_all, dy_out, stores.at[5])
    save_dy.start()
    for copy in flat_o:
        copy.wait_recv()
    save_wo = pltpu.make_async_copy(wo_all, wo_out, stores.at[6])
    save_wo.start()

    @pl.loop(0, 2)
    def _(step):
        at = pl.ds(pl.multiple_of(step * 2 * pair, 2 * pair), 2 * pair)
        to_heads[at, 3 * HD : 4 * HD] = dot(dy_all[at, :], wo_all[...], 1, 1).astype(bf16)

    for copy in swaps(1, to_heads, heads, o_cols):
        copy.start()
    keep_o = keep_own(3, to_heads, heads, o_cols)
    keep_o.start()

    grad_k[...] = jnp.zeros_like(grad_k)
    grad_v[...] = jnp.zeros_like(grad_v)
    scale = HD ** (-0.5)
    keep_qkv.wait()
    for copy in swaps(0, to_heads, heads, qkv_cols):
        copy.wait_recv()

    @pl.loop(0, n_plane)
    def _(part):
        at = pl.ds(pl.multiple_of(part * pair, pair), pair)
        places = place_head[at, 0:1]
        scores = dot(heads[at, 0:HD], heads[:, HD : 2 * HD], 1, 1) * scale
        scores = jnp.where(key_row[...] <= places, scores, -1e30)
        weights = jnp.exp(scores - jnp.max(scores, axis=-1, keepdims=True))
        share = weights / jnp.sum(weights, axis=-1, keepdims=True)
        probs[at, :] = share
        value = dot(share.astype(bf16), heads[:, 2 * HD : 3 * HD])
        attention[at, :] = value
        from_heads[at, 3 * HD : 4 * HD] = value.astype(bf16)

    for copy in swaps(2, from_heads, back, o_cols):
        copy.start()

    keep_o.wait()
    for copy in swaps(1, to_heads, heads, o_cols):
        copy.wait_recv()

    @pl.loop(0, n_plane)
    def _(step):
        turn_at = lax.rem(step + 1, n_plane)
        part = lax.rem(plane + turn_at, n_plane)
        at = pl.ds(pl.multiple_of(part * pair, pair), pair)
        grad_out = heads[at, 3 * HD : 4 * HD]
        delta = jnp.sum(grad_out.astype(f32) * attention[at, :], axis=-1, keepdims=True)
        grad_prob = dot(grad_out, heads[:, 2 * HD : 3 * HD], 1, 1)
        share = probs[at, :]
        dscore = (share * (grad_prob - delta)).astype(bf16)
        grad_q = dot(dscore, heads[:, HD : 2 * HD]) * scale
        from_heads[at, 0:HD] = turn(grad_q, cos_head[at, :], -sin_head[at, :]).astype(bf16)

        @pl.when(turn_at > 0)
        def _():
            swap(3, from_heads, back, q_cols, part, turn_at).start()

        grad_k[...] += dot(dscore, heads[at, 0:HD], 0, 0)
        grad_v[...] += dot(share.astype(bf16), grad_out, 0, 0)

    @pl.loop(0, n_plane)
    def _(step):
        turn_at = lax.rem(step + 1, n_plane)
        part = lax.rem(plane + turn_at, n_plane)
        at = pl.ds(pl.multiple_of(part * pair, pair), pair)
        turned = turn(grad_k[at, :] * scale, cos_head[at, :], -sin_head[at, :])
        from_heads[at, HD : 2 * HD] = turned.astype(bf16)
        from_heads[at, 2 * HD : 3 * HD] = grad_v[at, :].astype(bf16)

        @pl.when(turn_at > 0)
        def _():
            swap(4, from_heads, back, kv_cols, part, turn_at).start()

    keep_back = keep_own(2, from_heads, back, pl.ds(0, 4 * HD))
    keep_back.start()

    spread_d.finish()
    save_wd = pltpu.make_async_copy(wd_all, wd_out, stores.at[7])
    save_wd.start()

    @pl.loop(0, n_shard)
    def _(step):
        at = pl.ds(pl.multiple_of(step * pair, pair), pair)
        one[at, n_hid : 2 * n_hid] = (dot(dy_all[at, :], wd_all[...], 1, 1) * slope[at, :]).astype(
            bf16
        )

    save_gup = pltpu.make_async_copy(one.at[:, n_hid : 2 * n_hid], gup_out, stores.at[10])
    save_gup.start()
    keep_back.wait()
    again = (
        swaps(2, from_heads, back, o_cols)
        + swaps(3, from_heads, back, q_cols)
        + swaps(4, from_heads, back, kv_cols)
    )
    for copy in again:
        copy.wait_recv()
    save_back = pltpu.make_async_copy(back, back_out, stores.at[11])
    save_back.start()

    @pl.when(jnp.logical_not(spot.head_here))
    def _():
        to_head.wait_send()

    chain_x.finish_sends()
    chain_dy.finish_sends()
    for copy in cols_q + cols_u + cols_v + pos_push:
        copy.wait_send()
    for spread in [spread_d, spread_q, spread_u]:
        spread.finish_sends()
    again += swaps(0, to_heads, heads, qkv_cols) + swaps(1, to_heads, heads, o_cols)
    for copy in flat_v + flat_o + again:
        copy.wait_send()
    for copy in [
        save_vec,
        save_moments,
        save_x,
        save_two,
        save_wq,
        save_dy,
        save_wo,
        save_wd,
        save_wu,
        save_hid,
        save_gup,
        save_back,
    ]:
        copy.wait()


def forward_all(n_plane, n_shard, x, dy, pos, vec, freq, wq, wu, wd, wo):
    f32, bf16 = jnp.float32, jnp.bfloat16
    n_slice = 2 * n_shard
    block, width = x.shape
    rows_in, rows_down = wq.shape[0], wd.shape[0]
    group = n_slice * block
    n_hid = n_plane * rows_down
    cols_q = 3 * HD
    n_vec, lanes = vec.shape
    dma = pltpu.SemaphoreType.DMA
    vmem = pltpu.VMEM
    shape = jax.ShapeDtypeStruct
    anywhere = pl.BlockSpec(memory_space=pl.ANY)
    far, near = n_shard - 1, n_plane - 1
    return pl.pallas_call(
        partial(forward_kernel, n_plane, n_shard),
        out_shape=[
            shape((group, width), bf16),
            shape((group, width), bf16),
            shape((group, width), bf16),
            shape((group, width), bf16),
            shape((group, n_hid), bf16),
            shape((group, n_hid), bf16),
            shape((group, 4 * HD), bf16),
            shape((width, cols_q), bf16),
            shape((width, n_hid), bf16),
            shape((n_hid, width), bf16),
            shape((HD, width), bf16),
            shape((n_vec, width), f32),
            shape((group, block), f32),
        ],
        in_specs=[anywhere] * 4 + [pl.BlockSpec(memory_space=vmem)] + [anywhere] * 4,
        out_specs=[anywhere] * 13,
        scratch_shapes=[
            vmem((group, width), bf16),
            vmem((group, width), bf16),
            vmem((group, width), bf16),
            vmem((group, width), bf16),
            vmem((width, cols_q), bf16),
            vmem((width, n_hid), bf16),
            vmem((n_hid, width), bf16),
            vmem((HD, width), bf16),
            vmem((n_plane, n_slice, n_vec, lanes), f32),
            vmem((n_shard, *pos.shape), jnp.int32),
            vmem((n_vec, width), f32),
            vmem(wu.shape, f32),
            vmem(wd.shape, f32),
            vmem(wo.shape, f32),
            vmem((n_slice, rows_in, cols_q), bf16),
            vmem((n_slice, rows_in, n_hid), bf16),
            vmem(wo.shape, bf16),
            vmem((group, 4 * HD), bf16),
            vmem((group, 4 * HD), bf16),
            vmem((group, 4 * HD), bf16),
            vmem((group, 4 * HD), bf16),
            vmem((group, HD), f32),
            vmem((group, HD), f32),
            *([vmem((group, block), f32)] * 5),
            vmem((1, group), f32),
            vmem((group, group), f32),
            vmem((group, n_hid), f32),
            vmem((group, HD), f32),
            vmem((group, block), f32),
            dma((8,)),
            dma((13,)),
            dma((4,)),
            *([dma((2, n_shard))] * 8),
            dma((far,)),
            dma((far,)),
            dma((3, n_slice - 1)),
            dma((3, n_slice - 1)),
            dma((2, near)),
            dma((2, near)),
            dma((3, 4)),
            dma((3, 4)),
            dma((5, near)),
            dma((5, near)),
            dma,
            dma,
        ],
        compiler_params=pltpu.CompilerParams(
            collective_id=0, has_side_effects=True, vmem_limit_bytes=VMEM_BYTES
        ),
        name="forward_all",
    )(x, dy, pos, vec, freq, wq, wu, wd, wo)


def add_rows(target, terms, rows):
    columns = target.shape[1]
    chunk = min(rows, 64 if columns <= 1024 else 32)

    @pl.loop(0, rows // chunk)
    def _(step):
        at = pl.ds(pl.multiple_of(step * chunk, chunk), chunk)
        for start in range(0, columns, 256):
            cols = slice(start, start + 256)
            total = terms[0][at, cols].astype(jnp.float32)
            for term in terms[1:]:
                total = total + term[at, cols].astype(jnp.float32)
            target[at, cols] = total.astype(target.dtype)


def backward_kernel(
    n_plane,
    n_shard,
    x_ref,
    dy_ref,
    one_ref,
    two_ref,
    hid_ref,
    gup_ref,
    back_ref,
    wq_ref,
    wu_ref,
    wd_ref,
    wo_ref,
    vec_ref,
    moments_ref,
    out_sum,
    hat_sum,
    dq_sum,
    du_sum,
    dd_sum,
    do_sum,
    vec_sum,
    big_one,
    big_two,
    big_three,
    x_rows,
    hid,
    gup,
    back,
    wq,
    wo,
    vec,
    moments,
    rows_part,
    other_half,
    theirs,
    parts,
    q_part,
    u_part,
    o_part,
    v_part,
    q_in,
    u_in,
    d_in,
    o_in,
    v_in,
    o_mid,
    v_mid,
    v_end,
    loads,
    local,
    pair_sent,
    pair_here,
    rows_sent,
    rows_here,
    flat_sent,
    flat_here,
    sum_sent,
    sum_here,
    cols_sent,
    cols_here,
    head_sent,
    head_here,
    x_sem,
    free,
):
    spot = Spot(n_plane, n_shard)
    plane, core, shard, slot = spot.plane, spot.core, spot.shard, spot.slot
    f32, bf16 = jnp.float32, jnp.bfloat16
    n_slice = 2 * n_shard
    n_group, width = dy_ref.shape
    block = n_group // n_slice
    pair = 2 * block
    rows_down = width // n_slice
    cols_q = 3 * HD
    n_hid = hid_ref.shape[1]
    rows_plane = width // n_plane
    rows_in = rows_plane // n_slice

    def load(source, target, place):
        copy = pltpu.make_async_copy(source, target, loads.at[place])
        copy.start()
        return copy

    def plane_rows(ref, at):
        return ref.at[pl.ds(pl.multiple_of(at * pair, pair), pair)]

    load_two = load(two_ref, big_three, 0)
    load_hid = load(hid_ref, hid, 1)
    load_dy = load(dy_ref, big_one, 2)
    load_back = load(back_ref, back, 3)
    load_wo = load(wo_ref, wo, 4)
    load_wd = load(wd_ref, big_two, 5)
    load_gup = load(gup_ref, gup, 7)
    load_wq = load(wq_ref, wq, 8)
    load_vec = load(vec_ref, vec, 9)
    load_moments = load(moments_ref, moments, 10)
    spot.greet(spot.keeper())

    def flat(place, source, target):
        return [
            push(
                source(to),
                target.at[turn_at],
                flat_sent.at[place, turn_at],
                flat_here.at[place, turn_at],
                plane=to,
            )
            for turn_at, to in spot.planes()
        ]

    def at_plane(ref, size):
        return lambda to: ref.at[pl.ds(pl.multiple_of(to * size, size), size)]

    sum_u = Gather(spot, u_part, rows_plane, u_in, sum_sent.at[0], sum_here.at[0])
    sum_q = Gather(spot, q_part, rows_plane, q_in, sum_sent.at[1], sum_here.at[1])
    sum_d = Gather(spot, big_two, rows_down, d_in, sum_sent.at[2], sum_here.at[2])
    flat_o = flat(0, at_plane(o_part, rows_in), o_in)
    flat_v = flat(
        1,
        lambda to: v_part.at[:, pl.ds(pl.multiple_of(to * rows_plane, rows_plane), rows_plane)],
        v_in,
    )

    def weight_grad(left, right, target, columns):
        @pl.loop(0, left.shape[1] // 512)
        def _(step):
            at = pl.ds(pl.multiple_of(step * 512, 512), 512)
            turned = left[:, at].T
            for start in range(0, columns, n_group):
                cols = slice(start, min(start + n_group, columns))
                target[at, cols] = dot(turned, right[:, cols]).astype(bf16)

    sums = [
        RowSum(spot, rows_part.at[place], parts.at[place], rows_sent.at[place], rows_here.at[place])
        for place in range(2)
    ]

    def pair_push(place, seq):
        return push(
            other_half.at[seq],
            theirs.at[seq],
            pair_sent.at[place, seq],
            pair_here.at[place, seq],
            core=1 - core,
        )

    def put(place, seq, cols, total):
        first, second = total[:block], total[block:]
        rows_part[place, seq, :, cols] = jnp.where(core == 0, first, second).astype(bf16)
        other_half[seq, :, cols] = jnp.where(core == 0, second, first).astype(bf16)

    def add_pairs(place):
        @pl.loop(0, n_shard)
        def _(seq):
            pair_push(place, seq).wait_recv()
            held = rows_part.at[place, seq]
            add_rows(held, [held, theirs.at[seq]], block)

        sums[place].start()

    def add_shards(place, target):
        sums[place].finish(sums[place].rows(shard))
        copy = pltpu.make_async_copy(sums[place].rows(shard), target, local.at[2, 1 + place])
        copy.start()
        return copy

    def regroup(place, held, target, wide):
        base = pl.multiple_of(plane * rows_plane, rows_plane)
        parts_here = held.shape[1] // wide

        def rows(to, part):
            start = pl.multiple_of(base + to * rows_in, rows_in)
            return held.at[pl.ds(start, rows_in), pl.ds(part * wide, wide)]

        def lands(part):
            start = pl.multiple_of(part * width + slot * wide, wide)
            return target.at[:, pl.ds(start, wide)]

        copies = []
        for turn_at, device in spot.group():
            to = device["core"] * n_shard + device["shard"]
            for part in range(parts_here):
                copies.append(
                    push(
                        rows(to, part),
                        lands(part),
                        cols_sent.at[place, turn_at, part],
                        cols_here.at[place, turn_at, part],
                        **device,
                    )
                )
        keeps = [
            pltpu.make_async_copy(rows(slot, part), lands(part), local.at[place, part])
            for part in range(parts_here)
        ]
        for copy in copies + keeps:
            copy.start()
        return copies, keeps

    load_two.wait()
    load_gup.wait()
    weight_grad(big_three, gup, u_part, n_hid)
    sum_u.start()

    load_wu = [
        load(
            wu_ref.at[pl.ds(part * n_group, n_group)],
            big_three.at[:, pl.ds(part * n_hid, n_hid)],
            11 + part,
        )
        for part in range(width // n_group)
    ]

    load_hid.wait()
    load_back.wait()
    load_wo.wait()
    load_wd.wait()

    @pl.loop(0, n_shard)
    def _(seq):
        at = pl.ds(pl.multiple_of(seq * pair, pair), pair)
        for start in range(0, width, n_group):
            cols = slice(start, start + n_group)
            total = dot(back[at, cols_q : cols_q + HD], wo[:, cols])
            put(0, seq, cols, total + dot(hid[at, :], big_two[:, cols]))
        pair_push(0, seq).start()

    add_pairs(0)
    pl.semaphore_signal(free, inc=1, device_id=dict(core=1 - core), device_id_type=MESH)

    def x_load(seq):
        return pltpu.make_async_copy(plane_rows(x_ref, seq), x_rows, x_sem)

    x_load(0).start()
    v_part[...] = jnp.zeros_like(v_part)
    load_wq.wait()
    load_vec.wait()
    for copy in load_wu:
        copy.wait()
    load_moments.wait()
    for seq in range(n_shard):
        pair_push(0, seq).wait_send()
    pl.semaphore_wait(free, 1)

    def norm_rows(seq):
        at = pl.ds(pl.multiple_of(seq * pair, pair), pair)
        mean, scale = moments[at, 0:1], moments[at, 1:2]
        for start in range(0, width, 512):
            cols = slice(start, start + 512)
            up_rows = slice(start % n_group, start % n_group + 512)
            up_cols = slice(start // n_group * n_hid, (start // n_group + 1) * n_hid)
            grad_one = dot(back[at, 0:cols_q], wq[cols, :], 1, 1)
            grad_two = dot(gup[at, :], big_three[up_rows, up_cols], 1, 1)
            if start == 0:
                x_load(seq).wait()
            hat = (x_rows[:, cols].astype(f32) - mean) * scale
            v_part[0:1, cols] += jnp.sum(grad_one * hat, axis=0, keepdims=True)
            v_part[1:2, cols] += jnp.sum(grad_one, axis=0, keepdims=True)
            v_part[2:3, cols] += jnp.sum(grad_two * hat, axis=0, keepdims=True)
            v_part[3:4, cols] += jnp.sum(grad_two, axis=0, keepdims=True)
            put(1, seq, cols, grad_one * vec[0:1, cols] + grad_two * vec[2:3, cols])
        pair_push(1, seq).start()

        @pl.when(seq + 1 < n_shard)
        def _():
            x_load(seq + 1).start()


    @pl.loop(0, n_shard // 2)
    def _(seq):
        norm_rows(seq)

    sum_u.relay()
    sums[0].relay(1)

    @pl.loop(n_shard // 2, n_shard)
    def _(seq):
        norm_rows(seq)

    load_one = load(one_ref, big_three, 6)
    add_pairs(1)
    sum_u.finish()
    cols_u, keep_u = regroup(0, u_part, du_sum, rows_down)

    load_one.wait()
    weight_grad(big_three, back, q_part, cols_q)
    sum_q.start()
    sums[0].relay(2)
    sums[1].relay(1)

    load_dy.wait()
    weight_grad(hid, big_one, big_two, width)
    sum_q.relay()
    sum_d.start()
    attn = back[:, cols_q : cols_q + HD]
    half = width // 2
    for part in range(2):
        cols = slice(part * half, (part + 1) * half)
        o_part[:, cols] = dot(attn, big_one[:, cols], 0, 0).astype(bf16)
    for copy in flat_o:
        copy.start()

    own = pl.ds(pl.multiple_of((shard * 2 + core) * block, block), block)
    column_out = jnp.sum(big_one[own, :].astype(f32), axis=0, keepdims=True)
    v_part[7:8, :] = column_out
    v_part[12:13, :] = column_out
    lanes = pl.ds(pl.multiple_of(slot * HD, HD), HD)
    for part in range(3):
        cols = slice(part * HD, (part + 1) * HD)
        v_part[4 + part : 5 + part, lanes] = jnp.sum(
            back[:, cols].astype(f32), axis=0, keepdims=True
        )
    lanes = pl.ds(pl.multiple_of(slot * rows_down, rows_down), rows_down)
    for part in range(n_plane):
        cols = slice(part * rows_down, (part + 1) * rows_down)
        v_part[8 + part : 9 + part, lanes] = jnp.sum(
            gup[:, cols].astype(f32), axis=0, keepdims=True
        )
    for copy in flat_v:
        copy.start()
    sums[1].relay(2)
    save_out = add_shards(0, out_sum)
    sum_q.finish()
    cols_q_copies, keep_q = regroup(1, q_part, dq_sum, HD)
    save_hat = add_shards(1, hat_sum)
    sum_d.relay()

    for copy in flat_o:
        copy.wait_recv()
    mine = o_part.at[pl.ds(pl.multiple_of(plane * rows_in, rows_in), rows_in)]
    add_rows(o_mid, [mine] + [o_in.at[turn_at] for turn_at in range(n_plane - 1)], rows_in)
    to_owner = push(
        o_mid,
        do_sum,
        head_sent,
        head_here,
        plane=spot.owner_plane,
        core=spot.owner_core,
        shard=plane,
    )
    own_rows = pltpu.make_async_copy(o_mid, do_sum, head_sent)

    @pl.when(spot.head_here)
    def _():
        own_rows.start()

    @pl.when(jnp.logical_not(spot.head_here))
    def _():
        to_owner.start()

    for copy in flat_v:
        copy.wait_recv()
    total = v_part[:, pl.ds(pl.multiple_of(plane * rows_plane, rows_plane), rows_plane)]
    for turn_at in range(n_plane - 1):
        total = total + v_in[turn_at]
    v_mid[...] = total
    wide = 2 * rows_in

    def lanes_of(device):
        half_slot = device["core"] * n_shard + device["shard"]
        return pl.ds(pl.multiple_of(lax.div(half_slot, 2) * wide, wide), wide)

    v_end[slot] = v_mid[:, lanes_of(spot.turned(0))]
    cols_v = []
    for turn_at, device in spot.group():
        cols_v.append(
            push(
                v_mid.at[:, lanes_of(device)],
                v_end.at[slot],
                cols_sent.at[2, turn_at, 0],
                cols_here.at[2, turn_at, 0],
                **device,
            )
        )
    for copy in cols_v:
        copy.start()

    save_sums = [save_out, save_hat]
    sum_d.finish()
    save_d = pltpu.make_async_copy(sum_d.own(), dd_sum, local.at[2, 0])
    save_d.start()
    for copy in cols_v:
        copy.wait_recv()
    total = v_end[0]
    for other in range(1, n_slice):
        total = total + v_end[other]
    odd = lax.rem(slot, 2) == 1
    vec_sum[...] = jnp.where(odd, pltpu.roll(total, rows_in, 1), total)

    for copy in keep_u + keep_q:
        copy.wait()
    for copy in cols_u + cols_q_copies:
        copy.wait_recv()

    @pl.when(spot.head_here)
    def _():
        own_rows.wait()

    @pl.when(jnp.logical_not(spot.head_here))
    def _():
        to_owner.wait_recv()
        to_owner.wait_send()

    for seq in range(n_shard):
        pair_push(1, seq).wait_send()
    for place in range(2):
        sums[place].finish_sends()
    for copy in save_sums + [save_d]:
        copy.wait()
    for total in [sum_u, sum_q, sum_d]:
        total.finish_sends()
    for copy in flat_o + flat_v + cols_u + cols_q_copies + cols_v:
        copy.wait_send()


def backward_all(n_plane, n_shard, *arrays):
    x, dy, _, _, hid, _, back, wq, _, _, wo, vec, moments = arrays
    f32, bf16 = jnp.float32, jnp.bfloat16
    n_slice = 2 * n_shard
    group, width = dy.shape
    block = group // n_slice
    rows_down = width // n_slice
    rows_plane = width // n_plane
    rows_in = rows_plane // n_slice
    cols_q, n_hid = 3 * HD, hid.shape[1]
    n_vec = 16
    dma = pltpu.SemaphoreType.DMA
    vmem = pltpu.VMEM
    shape = jax.ShapeDtypeStruct
    near = n_plane - 1
    inside = pl.BlockSpec(memory_space=vmem)
    anywhere = pl.BlockSpec(memory_space=pl.ANY)
    return pl.pallas_call(
        partial(backward_kernel, n_plane, n_shard),
        out_shape=[
            shape((block, width), bf16),
            shape((block, width), bf16),
            shape((rows_in, n_slice * cols_q), bf16),
            shape((rows_in, n_slice * n_hid), bf16),
            shape((rows_down, width), bf16),
            shape((rows_in, width), bf16),
            shape((n_vec, 2 * rows_in), f32),
        ],
        in_specs=[anywhere] * 13,
        out_specs=[anywhere] * 6 + [inside],
        scratch_shapes=[
            vmem((group, width), bf16),
            vmem((group, width), bf16),
            vmem((group, width), bf16),
            vmem((2 * block, width), bf16),
            vmem(hid.shape, bf16),
            vmem(hid.shape, bf16),
            vmem(back.shape, bf16),
            vmem(wq.shape, bf16),
            vmem(wo.shape, bf16),
            vmem(vec.shape, f32),
            vmem(moments.shape, f32),
            vmem((2, n_shard, block, width), bf16),
            vmem((n_shard, block, width), bf16),
            vmem((n_shard, block, width), bf16),
            vmem((2, n_shard + 1, block, width), bf16),
            vmem((width, cols_q), bf16),
            vmem((width, n_hid), bf16),
            vmem(wo.shape, bf16),
            vmem((n_vec, width), f32),
            vmem((6, rows_plane // 2, cols_q), bf16),
            vmem((6, rows_plane // 2, n_hid), bf16),
            vmem((6, rows_down // 2, width), bf16),
            vmem((near, rows_in, width), bf16),
            vmem((near, n_vec, rows_plane), f32),
            vmem((rows_in, width), bf16),
            vmem((n_vec, rows_plane), f32),
            vmem((n_slice, n_vec, 2 * rows_in), f32),
            dma((13,)),
            dma((3, n_plane)),
            dma((2, n_shard)),
            dma((2, n_shard)),
            dma((2, 2, n_shard)),
            dma((2, 2, n_shard)),
            dma((2, near)),
            dma((2, near)),
            dma((3, 6)),
            dma((3, 6)),
            dma((3, n_slice - 1, n_plane)),
            dma((3, n_slice - 1, n_plane)),
            dma,
            dma,
            dma,
            pltpu.SemaphoreType.REGULAR,
        ],
        compiler_params=pltpu.CompilerParams(
            collective_id=1, has_side_effects=True, vmem_limit_bytes=VMEM_BYTES
        ),
        name="backward_all",
    )(*arrays)


def fast_device(
    layer_input,
    out_grad,
    positions,
    w_qkv,
    w_dense,
    w_up,
    w_down,
    vectors,
    m_qkv,
    m_dense,
    m_up,
    m_down,
    m_vectors,
    v_qkv,
    v_dense,
    v_up,
    v_down,
    v_vectors,
):
    bf16 = jnp.bfloat16
    f32 = jnp.float32
    n_plane = lax.axis_size("plane")
    n_shard = lax.axis_size("shard")
    block_rows = layer_input.shape[1]
    n_vec, vec_cols = vectors.shape

    half_rot = ROT // 2
    inverse = 10000.0 ** (-jnp.arange(0, ROT, 2).astype(f32) / ROT)
    freq = jnp.pad(jnp.concatenate([inverse, inverse]), (0, 128 - 2 * half_rot))[None]
    kept = forward_all(
        n_plane,
        n_shard,
        layer_input[0],
        out_grad[0],
        positions.reshape(-1, block_rows),
        jnp.pad(vectors, ((0, 16 - n_vec), (0, 128 - vec_cols))),
        freq,
        w_qkv,
        w_up,
        w_down,
        w_dense,
    )
    branches, grad_hat, part_qkv, part_up, part_down, part_dense, part_vec = backward_all(
        n_plane, n_shard, *kept
    )
    full_vec = kept[-2]
    branches = branches.astype(f32)
    grad_hat = grad_hat.astype(f32)
    own_tokens = layer_input[0].astype(f32)
    grad_rows = out_grad[0].astype(f32)
    layer_output = (own_tokens + branches + full_vec[7] + full_vec[12]).astype(bf16)[None]
    own_center = own_tokens - jnp.mean(own_tokens, axis=-1, keepdims=True)
    own_inv = lax.rsqrt(jnp.mean(own_center * own_center, axis=-1, keepdims=True) + 1e-05)
    own_hat = own_center * own_inv
    grad_input = (
        grad_rows
        + own_inv
        * (
            grad_hat
            - jnp.mean(grad_hat, axis=-1, keepdims=True)
            - own_hat * jnp.mean(grad_hat * own_hat, axis=-1, keepdims=True)
        )
    )[None]
    grad_vectors = part_vec[:n_vec, :vec_cols]
    grad_dense = part_dense.astype(f32)
    grad_down = part_down.astype(f32)
    grad_qkv = part_qkv.astype(f32)
    grad_up = part_up.astype(f32)
    new_qkv, second_qkv = adam_step(w_qkv, grad_qkv, m_qkv, v_qkv, 4.0 * (D // 2) ** (-0.5), 0.1)
    new_dense, second_dense = adam_step(
        w_dense, grad_dense, m_dense, v_dense, 4.0 * (D // 32) ** (-0.5), 0.1
    )
    new_up, second_up = adam_step(w_up, grad_up, m_up, v_up, 4.0 * D ** (-0.5), 0.1)
    new_down, second_down = adam_step(w_down, grad_down, m_down, v_down, 4.0 * FF ** (-0.5), 0.1)
    new_vectors, second_vectors = adam_step(vectors, grad_vectors, m_vectors, v_vectors, 1.0, 0.0)
    return (
        layer_output,
        grad_input,
        grad_qkv,
        grad_dense,
        grad_up,
        grad_down,
        grad_vectors,
        second_qkv,
        second_dense,
        second_up,
        second_down,
        second_vectors,
        new_qkv,
        new_dense,
        new_up,
        new_down,
        new_vectors,
    )


def solution(mesh):
    n_ctx, n_shard = mesh.devices.shape
    if n_ctx == 2 * n_shard and n_ctx == H:
        device_mesh = Mesh(
            mesh.devices.reshape(n_shard, 2, n_shard), ("plane", "core", "shard")
        )
        ctx, body = ("plane", "core"), fast_device
    else:
        device_mesh, ctx, body = mesh, ("ctx",), general_device
    rows = P("shard", ctx, None)
    weight = P((*ctx, "shard"), None)
    vector = P(None, (*ctx, "shard"))
    matrices = (weight,) * 4 + (vector,)
    in_specs = (rows, rows, P("shard", None)) + matrices * 3
    out_specs = (rows, rows) + matrices * 3
    return jax.shard_map(
        body, mesh=device_mesh, in_specs=in_specs, out_specs=out_specs, check_vma=False
    )
```

profile of v0, /device:TPU:18, one launch (start us, length us, event | category | flops | bytes accessed | tf_op | source)
XLA Modules:
  0.0 343.4 jit_solution(14165948302764737533)
XLA Ops:
  0.7 1.3 pad.8.vec_ref
  2.0 0.6 fusion.19.freq_ref
  2.6 174.6 %forward_all.1 = (bf16[1024,2048]{1,0:T(8,128)(2,1)}, bf16[1024,2048]{1,0:T(8,128)(2,1)}, bf16[1024,2048]{1,0:T(8,128)(2,1)}, bf16[1024,2048]{1,0:T(8,128)(2,1)}...) custom-call(bf16[128,2048]{1,0:T(8,128)(2,1)} %bitcast.17, ...), custom_call_target="tpu_custom_call" | custom-call | tf_op jit(solution)/shard_map/forward_all/pallas_call | solution.py:1273
  177.2 146.5 %backward_all.1 = (bf16[128,2048]{1,0:T(8,128)(2,1)}, bf16[128,2048]{1,0:T(8,128)(2,1)}, bf16[64,6144]{1,0:T(8,128)(2,1)}, bf16[64,8192]{1,0:T(8,128)(2,1)}, bf1...) custom-call(bf16[1024,2048]{1,0:T(8,128)(2,1)} %get-tuple-element.37.x_ref, ...), custom_call_target="tpu_custom_call" | custom-call | tf_op jit(solution)/shard_map/backward_all/pallas_call | solution.py:1795
  323.6 0.0 copy-start.1
  323.6 0.0 copy-start.4
  323.7 0.0 copy-start.5
  323.7 0.0 copy-start.10
  323.7 6.7 %multiply_subtract_fusion = (f32[256,2048]{1,0:T(8,128)}, f32[256,2048]{1,0:T(8,128)}, f32[256,2048]{1,0:T(8,128)}) fusion(f32[256,2048]{1,0:T(8,128)} %wd_ref.1, f32[256,2048]{1,0:T(8,128)} %param.29, f32[256,2048]{1,0:T(8,128)} %param.34, bf16[256,2048]{1,0:T(8,128)(2,1)} %get-tuple-element.55), kind=kLoop, calls=%fused_computation.5 | loop fusion | flops 8388608 | bytes 13631488 | tf_op jit(solution)/shard_map/sub | solution.py:53
  330.3 0.0 copy-done.1
  330.3 0.0 copy-done.4
  330.3 0.0 copy-done.5
  330.3 0.0 copy-done.10
  330.4 0.0 copy-start.2
  330.4 0.0 copy-start.8
  330.4 0.0 copy-start.9
  330.4 0.0 copy-start.11
  330.4 3.7 %multiply_subtract_fusion.1 = (f32[64,8192]{1,0:T(8,128)}, f32[64,8192]{1,0:T(8,128)}, f32[64,8192]{1,0:T(8,128)}) fusion(f32[64,8192]{1,0:T(8,128)S(1)} %copy-done.1, f32[64,8192]{1,0:T(8,128)S(1)} %copy-done.4, f32[64,8192]{1,0:T(8,128)S(1)} %copy-done.5, bf16[64,8192]{1,0:T(8,128)(2,1)S(1)} %copy-done.10), kind=kLoop, calls=%fused_computation.6 | loop fusion | flops 8388608 | bytes 13631488 | tf_op jit(solution)/shard_map/sub | solution.py:53
  334.1 0.7 copy-done.9
  334.8 0.3 copy-done.11
  335.1 2.6 multiply_subtract_fusion.2
  337.7 0.2 convert_reduce_fusion.1
  337.9 0.3 fusion.10
  338.2 0.4 convert_reduce_fusion
  338.6 0.0 copy-start.13
  338.6 0.0 copy-start.14
  338.6 0.0 copy-start.15
  338.6 1.0 fusion.25
  339.6 1.8 fusion.9
  341.5 1.3 multiply_subtract_fusion.3
  342.8 0.0 copy-done.17
  342.8 0.6 add_subtract_fusion
  (26 shorter events, 0.1 us)
Async XLA Ops:
  323.6 6.7 %copy-start.1 = (f32[64,8192]{1,0:T(8,128)S(1)}, f32[64,8192]{1,0:T(8,128)}, u32[]{:S(2)}) copy-start(f32[64,8192]{1,0:T(8,128)} %wu_ref.1) | copy-start | bytes 6291460
  323.6 6.7 %copy-start.4 = (f32[64,8192]{1,0:T(8,128)S(1)}, f32[64,8192]{1,0:T(8,128)}, u32[]{:S(2)}) copy-start(f32[64,8192]{1,0:T(8,128)} %param.28) | copy-start | bytes 6291460
  323.7 6.7 %copy-start.5 = (f32[64,8192]{1,0:T(8,128)S(1)}, f32[64,8192]{1,0:T(8,128)}, u32[]{:S(2)}) copy-start(f32[64,8192]{1,0:T(8,128)} %param.33) | copy-start | bytes 6291460
  323.7 6.7 %copy-start.10 = (bf16[64,8192]{1,0:T(8,128)(2,1)S(1)}, bf16[64,8192]{1,0:T(8,128)(2,1)}, u32[]{:S(2)}) copy-start(bf16[64,8192]{1,0:T(8,128)(2,1)} %get-tuple-element.54) | copy-start | bytes 3145732
  330.4 3.7 %copy-start.2 = (f32[64,6144]{1,0:T(8,128)S(1)}, f32[64,6144]{1,0:T(8,128)}, u32[]{:S(2)}) copy-start(f32[64,6144]{1,0:T(8,128)} %wq_ref.1) | copy-start | bytes 4718596
  330.4 3.7 %copy-start.8 = (f32[64,6144]{1,0:T(8,128)S(1)}, f32[64,6144]{1,0:T(8,128)}, u32[]{:S(2)}) copy-start(f32[64,6144]{1,0:T(8,128)} %param.26) | copy-start | bytes 4718596
  330.4 4.4 %copy-start.9 = (f32[64,6144]{1,0:T(8,128)S(1)}, f32[64,6144]{1,0:T(8,128)}, u32[]{:S(2)}) copy-start(f32[64,6144]{1,0:T(8,128)} %param.31) | copy-start | bytes 4718596
  330.4 4.7 %copy-start.11 = (bf16[64,6144]{1,0:T(8,128)(2,1)S(1)}, bf16[64,6144]{1,0:T(8,128)(2,1)}, u32[]{:S(2)}) copy-start(bf16[64,6144]{1,0:T(8,128)(2,1)} %get-tuple-element.52) | copy-start | bytes 2359300
  335.1 2.6 copy-start
  335.1 3.0 copy-start.3
  337.7 1.9 copy-start.6
  337.7 1.9 copy-start.12
  338.6 2.9 copy-start.7
  338.6 2.9 copy-start.13
  338.6 2.9 copy-start.14
  338.6 2.9 copy-start.15
  341.4 1.3 copy-start.16
  341.4 1.3 copy-start.17
  341.4 1.3 copy-start.18
  341.4 1.3 copy-start.19
where the time goes:
time: 344 us; the launch traced here: 343 us
  Pallas kernels  321 us (93%)
  other arithmetic  18 us (5%)
  local copies, waits for them, and re-layouts  3.47 us (1%)
    pallas_call x1, Pallas kernels, forward_all(): pl.pallas_call(partial(forward_kernel, n_plane, n_shard), out_shape=[shap...  175 us
    pallas_call x1, Pallas kernels, backward_all(): pl.pallas_call(partial(backward_kernel, n_plane, n_shard), out_shape=[sha...  146 us
    sub x5, other arithmetic, adam_step(): weight - rate * (unbiased / (jnp.sqrt(scaled) + 1e-08) + decay * weight)  14.8 us

commit v1 on v0

--- a/solution.py
+++ b/solution.py
@@ -949,18 +949,6 @@
     def _():
         to_head.start()
 
-    raw[5].wait()
-    chain_x.step(1)
-    for copy in cols_u:
-        copy.start()
-    spread_d.relay()
-    chain_dy.start()
-    keep_q.wait()
-    for copy in cols_q:
-        copy.wait_recv()
-    spread_q.start()
-    chain_x.step(2)
-
     for copy in pos_push:
         copy.wait_recv()
     freq = freq_ref[...]
@@ -974,38 +962,7 @@
             cos_row[at, :] = cosine
             sin_row[at, :] = sine
 
-    spread_q.relay()
-    keep_u.wait()
-    for copy in cols_u:
-        copy.wait_recv()
-    spread_u.start()
-    chain_dy.step(1)
-    for dist in range(3, n_shard):
-        chain_x.step(dist)
-
-    @pl.when(spot.head_here)
-    def _():
-        own_head.wait()
-
-    @pl.when(jnp.logical_not(spot.head_here))
-    def _():
-        to_head.wait_recv()
-
-    for copy in flat_o:
-        copy.start()
-
-    @pl.loop(0, n_plane)
-    def _(part):
-        for half in range(2):
-            at = pl.ds(pl.multiple_of(part * pair + half * block, block), block)
-            cosine, sine, places = turn_tables(pos_all[plane, pl.ds(2 * part + half, 1), :], freq)
-            cos_head[at, :] = cosine
-            sin_head[at, :] = sine
-            place_head[at, :] = places
-
-    for at in range(pos_all.shape[1]):
-        key_row[:, at * block : (at + 1) * block] = pos_all[plane, pl.ds(at, 1), :].astype(f32)
-
+    raw[5].wait()
     for copy in flat_v:
         copy.wait_recv()
     n_vec, lanes = vec_all.shape[2:]
@@ -1018,10 +975,6 @@
             )
     save_vec = pltpu.make_async_copy(full_vec, vec_out, stores.at[0])
     save_vec.start()
-
-    chain_x.finish_pairs()
-    save_x = pltpu.make_async_copy(x_all, x_out, stores.at[1])
-    save_x.start()
 
     def norm_rows(seq):
         @pl.loop(0, pair // 32)
@@ -1037,11 +990,68 @@
             one[at, :] = (hat * full_vec[0:1, :] + full_vec[1:2, :]).astype(bf16)
             two[at, :] = (hat * full_vec[2:3, :] + full_vec[3:4, :]).astype(bf16)
 
-    for seq in range(n_shard):
-        norm_rows(seq)
-        if seq == 1:
-            chain_dy.step(2)
-            spread_u.relay()
+    def norm_came(dist):
+        for side in range(2):
+
+            @pl.when(chain_x.holds(side, dist))
+            def _():
+                chain_x.pair(side, dist).wait_recv()
+                norm_rows(shard - dist if side == 0 else shard + dist)
+
+    chain_x.step(1)
+    for copy in cols_u:
+        copy.start()
+    chain_x.pair(0, 0).wait_recv()
+    norm_rows(shard)
+    spread_d.relay()
+    keep_q.wait()
+    for copy in cols_q:
+        copy.wait_recv()
+    spread_q.start()
+    norm_came(1)
+    chain_x.step(2)
+    chain_dy.start()
+    spread_q.relay()
+    norm_came(2)
+    keep_u.wait()
+    for copy in cols_u:
+        copy.wait_recv()
+    spread_u.start()
+
+    @pl.loop(0, n_plane)
+    def _(part):
+        for half in range(2):
+            at = pl.ds(pl.multiple_of(part * pair + half * block, block), block)
+            cosine, sine, places = turn_tables(pos_all[plane, pl.ds(2 * part + half, 1), :], freq)
+            cos_head[at, :] = cosine
+            sin_head[at, :] = sine
+            place_head[at, :] = places
+
+    for at in range(pos_all.shape[1]):
+        key_row[:, at * block : (at + 1) * block] = pos_all[plane, pl.ds(at, 1), :].astype(f32)
+
+    for dist in range(3, n_shard):
+        chain_x.step(dist)
+
+    @pl.when(spot.head_here)
+    def _():
+        own_head.wait()
+
+    @pl.when(jnp.logical_not(spot.head_here))
+    def _():
+        to_head.wait_recv()
+
+    for copy in flat_o:
+        copy.start()
+
+
+    chain_dy.step(1)
+    for dist in range(3, n_shard):
+        norm_came(dist)
+    save_x = pltpu.make_async_copy(x_all, x_out, stores.at[1])
+    save_x.start()
+    spread_u.relay()
+    chain_dy.step(2)
     save_moments = pltpu.make_async_copy(moments, moments_out, stores.at[12])
     save_moments.start()
     save_one = pltpu.make_async_copy(one, one_out, stores.at[2])
@@ -1111,12 +1121,16 @@
             slope[at, cols] = half + value * (0.3989422804014327 * jnp.exp(-0.5 * value * value))
             one[at, cols] = (value * half).astype(bf16)
 
-    @pl.loop(0, n_shard)
+    @pl.loop(0, n_shard // 2)
     def _(step):
         hidden_rows(step)
 
     for dist in range(3, n_shard):
         chain_dy.step(dist)
+
+    @pl.loop(n_shard // 2, n_shard)
+    def _(step):
+        hidden_rows(step)
 
     save_hid = pltpu.make_async_copy(one.at[:, 0:n_hid], hid_out, stores.at[9])
     save_hid.start()
@@ -1851,7 +1865,7 @@
             pltpu.SemaphoreType.REGULAR,
         ],
         compiler_params=pltpu.CompilerParams(
-            collective_id=1, has_side_effects=True, vmem_limit_bytes=VMEM_BYTES
+            collective_id=1, has_side_effects=True, vmem_limit_bytes=59 * 1024 * 1024
         ),
         name="backward_all",
     )(*arrays)

time: 344 us -> 343 us (level)
  no operation moved by 1% of the time
where the time goes in v1:
time: 343 us; the launch traced here: 342 us
  Pallas kernels  321 us (94%)
  other arithmetic  16.8 us (5%)
  local copies, waits for them, and re-layouts  3.48 us (1%)
    pallas_call x1, Pallas kernels, forward_all(): pl.pallas_call(partial(forward_kernel, n_plane, n_shard), out_shape=[shap...  174 us
    pallas_call x1, Pallas kernels, backward_all(): pl.pallas_call(partial(backward_kernel, n_plane, n_shard), out_shape=[sha...  147 us
    sub x5, other arithmetic, adam_step(): weight - rate * (unbiased / (jnp.sqrt(scaled) + 1e-08) + decay * weight)  13.5 us

profile of v1, /device:TPU:18, one launch (start us, length us, event | category | flops | bytes accessed | tf_op | source)
XLA Modules:
  0.0 342.3 jit_solution(6411667277806666238)
XLA Ops:
  0.7 1.3 pad.8.vec_ref
  2.0 0.6 fusion.19.freq_ref
  2.6 174.0 %forward_all.1 = (bf16[1024,2048]{1,0:T(8,128)(2,1)}, bf16[1024,2048]{1,0:T(8,128)(2,1)}, bf16[1024,2048]{1,0:T(8,128)(2,1)}, bf16[1024,2048]{1,0:T(8,128)(2,1)}...) custom-call(bf16[128,2048]{1,0:T(8,128)(2,1)} %bitcast.17, ...), custom_call_target="tpu_custom_call" | custom-call | tf_op jit(solution)/shard_map/forward_all/pallas_call | solution.py:1287
  176.5 0.0 copy-start.1
  176.5 0.0 copy-start.5
  176.5 147.2 %backward_all.1 = (bf16[128,2048]{1,0:T(8,128)(2,1)}, bf16[128,2048]{1,0:T(8,128)(2,1)}, bf16[64,6144]{1,0:T(8,128)(2,1)}, bf16[64,8192]{1,0:T(8,128)(2,1)}, bf1...) custom-call(bf16[1024,2048]{1,0:T(8,128)(2,1)} %get-tuple-element.37.x_ref, ...), custom_call_target="tpu_custom_call" | custom-call | tf_op jit(solution)/shard_map/backward_all/pallas_call | solution.py:1809
  323.7 0.0 copy-done.1
  323.7 0.0 copy-start.2
  323.7 0.0 copy-start.6
  323.8 0.0 copy-start.7
  323.8 0.0 copy-start.12
  323.8 5.4 %multiply_subtract_fusion = (f32[256,2048]{1,0:T(8,128)}, f32[256,2048]{1,0:T(8,128)}, f32[256,2048]{1,0:T(8,128)}) fusion(f32[256,2048]{1,0:T(8,128)S(1)} %copy-done.1, f32[256,2048]{1,0:T(8,128)S(1)} %copy-done.5, f32[256,2048]{1,0:T(8,128)} %param.34, bf16[256,2048]{1,0:T(8,128)(2,1)} %get-tuple-element.55), kind=kLoop, calls=%fused_computation.5 | loop fusion | flops 8388608 | bytes 13631488 | tf_op jit(solution)/shard_map/sub | solution.py:53
  329.2 0.0 copy-done.6
  329.2 0.0 copy-start.3
  329.2 0.0 copy-start.10
  329.2 0.0 copy-start.11
  329.3 3.7 %multiply_subtract_fusion.1 = (f32[64,8192]{1,0:T(8,128)}, f32[64,8192]{1,0:T(8,128)}, f32[64,8192]{1,0:T(8,128)}) fusion(f32[64,8192]{1,0:T(8,128)S(1)} %copy-done.2, f32[64,8192]{1,0:T(8,128)S(1)} %copy-done.6, f32[64,8192]{1,0:T(8,128)S(1)} %copy-done.7, bf16[64,8192]{1,0:T(8,128)(2,1)S(1)} %copy-done.12), kind=kLoop, calls=%fused_computation.6 | loop fusion | flops 8388608 | bytes 13631488 | tf_op jit(solution)/shard_map/sub | solution.py:53
  332.9 0.0 copy-done.3
  332.9 0.7 copy-done.11
  333.6 0.3 copy-done.13
  334.0 2.6 multiply_subtract_fusion.2
  336.6 0.2 convert_reduce_fusion.1
  336.7 0.3 fusion.10
  337.0 0.4 convert_reduce_fusion
  337.4 0.0 copy-start.15
  337.4 0.0 copy-start.16
  337.4 0.0 copy-start.17
  337.5 1.0 fusion.25
  338.5 1.8 fusion.9
  340.4 1.3 multiply_subtract_fusion.3
  341.6 0.0 copy-done.19
  341.6 0.6 add_subtract_fusion
  (30 shorter events, 0.1 us)
Async XLA Ops:
  176.5 147.2 %copy-start.1 = (f32[256,2048]{1,0:T(8,128)S(1)}, f32[256,2048]{1,0:T(8,128)}, u32[]{:S(2)}) copy-start(f32[256,2048]{1,0:T(8,128)} %wd_ref.1) | copy-start | bytes 6291460
  176.5 147.2 %copy-start.5 = (f32[256,2048]{1,0:T(8,128)S(1)}, f32[256,2048]{1,0:T(8,128)}, u32[]{:S(2)}) copy-start(f32[256,2048]{1,0:T(8,128)} %param.29) | copy-start | bytes 6291460
  323.7 5.5 %copy-start.2 = (f32[64,8192]{1,0:T(8,128)S(1)}, f32[64,8192]{1,0:T(8,128)}, u32[]{:S(2)}) copy-start(f32[64,8192]{1,0:T(8,128)} %wu_ref.1) | copy-start | bytes 6291460
  323.7 5.5 %copy-start.6 = (f32[64,8192]{1,0:T(8,128)S(1)}, f32[64,8192]{1,0:T(8,128)}, u32[]{:S(2)}) copy-start(f32[64,8192]{1,0:T(8,128)} %param.28) | copy-start | bytes 6291460
  323.8 5.5 %copy-start.7 = (f32[64,8192]{1,0:T(8,128)S(1)}, f32[64,8192]{1,0:T(8,128)}, u32[]{:S(2)}) copy-start(f32[64,8192]{1,0:T(8,128)} %param.33) | copy-start | bytes 6291460
  323.8 5.4 %copy-start.12 = (bf16[64,8192]{1,0:T(8,128)(2,1)S(1)}, bf16[64,8192]{1,0:T(8,128)(2,1)}, u32[]{:S(2)}) copy-start(bf16[64,8192]{1,0:T(8,128)(2,1)} %get-tuple-element.54) | copy-start | bytes 3145732
  329.2 3.7 %copy-start.3 = (f32[64,6144]{1,0:T(8,128)S(1)}, f32[64,6144]{1,0:T(8,128)}, u32[]{:S(2)}) copy-start(f32[64,6144]{1,0:T(8,128)} %wq_ref.1) | copy-start | bytes 4718596
  329.2 3.7 %copy-start.10 = (f32[64,6144]{1,0:T(8,128)S(1)}, f32[64,6144]{1,0:T(8,128)}, u32[]{:S(2)}) copy-start(f32[64,6144]{1,0:T(8,128)} %param.26) | copy-start | bytes 4718596
  329.2 4.4 %copy-start.11 = (f32[64,6144]{1,0:T(8,128)S(1)}, f32[64,6144]{1,0:T(8,128)}, u32[]{:S(2)}) copy-start(f32[64,6144]{1,0:T(8,128)} %param.31) | copy-start | bytes 4718596
  329.3 4.7 %copy-start.13 = (bf16[64,6144]{1,0:T(8,128)(2,1)S(1)}, bf16[64,6144]{1,0:T(8,128)(2,1)}, u32[]{:S(2)}) copy-start(bf16[64,6144]{1,0:T(8,128)(2,1)} %get-tuple-element.52) | copy-start | bytes 2359300
  334.0 2.6 copy-start
  334.0 3.0 copy-start.4
  336.5 1.9 copy-start.8
  336.6 1.9 copy-start.14
  337.4 2.9 copy-start.9
  337.4 2.9 copy-start.15
  337.4 2.9 copy-start.16
  337.4 2.9 copy-start.17
  340.3 1.3 copy-start.18
  340.3 1.3 copy-start.19
  340.3 1.3 copy-start.20
  340.3 1.3 copy-start.21

commit v2 on v1

--- a/solution.py
+++ b/solution.py
@@ -789,7 +789,6 @@
     sin_row,
     key_row,
     probs,
-    slope,
     attention,
     moments,
     loads,
@@ -1004,19 +1003,15 @@
     chain_x.pair(0, 0).wait_recv()
     norm_rows(shard)
     spread_d.relay()
+    chain_dy.start()
     keep_q.wait()
     for copy in cols_q:
         copy.wait_recv()
     spread_q.start()
     norm_came(1)
     chain_x.step(2)
-    chain_dy.start()
     spread_q.relay()
     norm_came(2)
-    keep_u.wait()
-    for copy in cols_u:
-        copy.wait_recv()
-    spread_u.start()
 
     @pl.loop(0, n_plane)
     def _(part):
@@ -1050,7 +1045,10 @@
         norm_came(dist)
     save_x = pltpu.make_async_copy(x_all, x_out, stores.at[1])
     save_x.start()
-    spread_u.relay()
+    keep_u.wait()
+    for copy in cols_u:
+        copy.wait_recv()
+    spread_u.start()
     chain_dy.step(2)
     save_moments = pltpu.make_async_copy(moments, moments_out, stores.at[12])
     save_moments.start()
@@ -1104,36 +1102,8 @@
     keep_qkv = keep_own(2, to_heads, heads, qkv_cols)
     keep_qkv.start()
 
-    spread_u.finish()
-    save_wu = pltpu.make_async_copy(wu_all, wu_out, stores.at[8])
-    save_wu.start()
-    save_one.wait()
-    up_lanes = pl.ds(pl.multiple_of(slot * rows_down, rows_down), rows_down)
-    n_hid = n_plane * rows_down
-
-    def hidden_rows(step):
-        at = pl.ds(pl.multiple_of(step * pair, pair), pair)
-        hidden = dot(two[at, :], wu_all[...])
-        for part in range(n_plane):
-            cols = slice(part * rows_down, (part + 1) * rows_down)
-            value = hidden[:, cols] + full_vec[8 + part : 9 + part, up_lanes]
-            half = 0.5 + 0.5 * lax.erf(value * 0.7071067811865476)
-            slope[at, cols] = half + value * (0.3989422804014327 * jnp.exp(-0.5 * value * value))
-            one[at, cols] = (value * half).astype(bf16)
-
-    @pl.loop(0, n_shard // 2)
-    def _(step):
-        hidden_rows(step)
-
     for dist in range(3, n_shard):
         chain_dy.step(dist)
-
-    @pl.loop(n_shard // 2, n_shard)
-    def _(step):
-        hidden_rows(step)
-
-    save_hid = pltpu.make_async_copy(one.at[:, 0:n_hid], hid_out, stores.at[9])
-    save_hid.start()
 
     chain_dy.finish_pairs()
     save_dy = pltpu.make_async_copy(dy_all, dy_out, stores.at[5])
@@ -1176,6 +1146,8 @@
     for copy in swaps(2, from_heads, back, o_cols):
         copy.start()
 
+    spread_u.relay()
+
     keep_o.wait()
     for copy in swaps(1, to_heads, heads, o_cols):
         copy.wait_recv()
@@ -1216,17 +1188,32 @@
     keep_back = keep_own(2, from_heads, back, pl.ds(0, 4 * HD))
     keep_back.start()
 
+    spread_u.finish()
+    save_wu = pltpu.make_async_copy(wu_all, wu_out, stores.at[8])
+    save_wu.start()
     spread_d.finish()
     save_wd = pltpu.make_async_copy(wd_all, wd_out, stores.at[7])
     save_wd.start()
+    save_one.wait()
+    up_lanes = pl.ds(pl.multiple_of(slot * rows_down, rows_down), rows_down)
+    n_hid = n_plane * rows_down
 
     @pl.loop(0, n_shard)
     def _(step):
         at = pl.ds(pl.multiple_of(step * pair, pair), pair)
-        one[at, n_hid : 2 * n_hid] = (dot(dy_all[at, :], wd_all[...], 1, 1) * slope[at, :]).astype(
-            bf16
-        )
-
+        hidden = dot(two[at, :], wu_all[...])
+        grad = dot(dy_all[at, :], wd_all[...], 1, 1)
+        for part in range(n_plane):
+            cols = slice(part * rows_down, (part + 1) * rows_down)
+            grad_cols = slice(n_hid + part * rows_down, n_hid + (part + 1) * rows_down)
+            value = hidden[:, cols] + full_vec[8 + part : 9 + part, up_lanes]
+            half = 0.5 + 0.5 * lax.erf(value * 0.7071067811865476)
+            slope = half + value * (0.3989422804014327 * jnp.exp(-0.5 * value * value))
+            one[at, cols] = (value * half).astype(bf16)
+            one[at, grad_cols] = (grad[:, cols] * slope).astype(bf16)
+
+    save_hid = pltpu.make_async_copy(one.at[:, 0:n_hid], hid_out, stores.at[9])
+    save_hid.start()
     save_gup = pltpu.make_async_copy(one.at[:, n_hid : 2 * n_hid], gup_out, stores.at[10])
     save_gup.start()
     keep_back.wait()
@@ -1330,7 +1317,6 @@
             *([vmem((group, block), f32)] * 5),
             vmem((1, group), f32),
             vmem((group, group), f32),
-            vmem((group, n_hid), f32),
             vmem((group, HD), f32),
             vmem((group, block), f32),
             dma((8,)),

time: 343 us -> 350 us (1.020)
  Pallas kernels: 321 us -> 329 us
    pallas_call x1, Pallas kernels: 147 us -> 154 us  [backward_all(): pl.pallas_call(partial(backward_kernel, n_plane, n_shard), out_shape=[sha...]
where the time goes in v2:
time: 350 us
  Pallas kernels  329 us (94%)
  other arithmetic  16.8 us (5%)
    pallas_call x1, Pallas kernels, forward_all(): pl.pallas_call(partial(forward_kernel, n_plane, n_shard), out_shape=[shap...  175 us
    pallas_call x1, Pallas kernels, backward_all(): pl.pallas_call(partial(backward_kernel, n_plane, n_shard), out_shape=[sha...  154 us
    sub x5, other arithmetic, adam_step(): weight - rate * (unbiased / (jnp.sqrt(scaled) + 1e-08) + decay * weight)  13.5 us

profile of v2, /device:TPU:18, one launch (start us, length us, event | category | flops | bytes accessed | tf_op | source)
XLA Modules:
  0.0 349.7 jit_solution(17638317921986094873)
XLA Ops:
  0.7 1.3 pad.8.vec_ref
  2.0 0.6 fusion.19.freq_ref
  2.6 174.8 %forward_all.1 = (bf16[1024,2048]{1,0:T(8,128)(2,1)}, bf16[1024,2048]{1,0:T(8,128)(2,1)}, bf16[1024,2048]{1,0:T(8,128)(2,1)}, bf16[1024,2048]{1,0:T(8,128)(2,1)}...) custom-call(bf16[128,2048]{1,0:T(8,128)(2,1)} %bitcast.17, ...), custom_call_target="tpu_custom_call" | custom-call | tf_op jit(solution)/shard_map/forward_all/pallas_call | solution.py:1274
  177.3 0.0 copy-start.1
  177.3 0.0 copy-start.5
  177.3 153.8 %backward_all.1 = (bf16[128,2048]{1,0:T(8,128)(2,1)}, bf16[128,2048]{1,0:T(8,128)(2,1)}, bf16[64,6144]{1,0:T(8,128)(2,1)}, bf16[64,8192]{1,0:T(8,128)(2,1)}, bf1...) custom-call(bf16[1024,2048]{1,0:T(8,128)(2,1)} %get-tuple-element.37.x_ref, ...), custom_call_target="tpu_custom_call" | custom-call | tf_op jit(solution)/shard_map/backward_all/pallas_call | solution.py:1795
  331.1 0.0 copy-done.1
  331.1 0.0 copy-done.5
  331.1 0.0 copy-start.2
  331.1 0.0 copy-start.6
  331.2 0.0 copy-start.7
  331.2 0.0 copy-start.12
  331.2 5.4 %multiply_subtract_fusion = (f32[256,2048]{1,0:T(8,128)}, f32[256,2048]{1,0:T(8,128)}, f32[256,2048]{1,0:T(8,128)}) fusion(f32[256,2048]{1,0:T(8,128)S(1)} %copy-done.1, f32[256,2048]{1,0:T(8,128)S(1)} %copy-done.5, f32[256,2048]{1,0:T(8,128)} %param.34, bf16[256,2048]{1,0:T(8,128)(2,1)} %get-tuple-element.55), kind=kLoop, calls=%fused_computation.5 | loop fusion | flops 8388608 | bytes 13631488 | tf_op jit(solution)/shard_map/sub | solution.py:53
  336.6 0.0 copy-done.6
  336.6 0.0 copy-start.3
  336.6 0.0 copy-start.10
  336.6 0.0 copy-start.11
  336.7 3.7 %multiply_subtract_fusion.1 = (f32[64,8192]{1,0:T(8,128)}, f32[64,8192]{1,0:T(8,128)}, f32[64,8192]{1,0:T(8,128)}) fusion(f32[64,8192]{1,0:T(8,128)S(1)} %copy-done.2, f32[64,8192]{1,0:T(8,128)S(1)} %copy-done.6, f32[64,8192]{1,0:T(8,128)S(1)} %copy-done.7, bf16[64,8192]{1,0:T(8,128)(2,1)S(1)} %copy-done.12), kind=kLoop, calls=%fused_computation.6 | loop fusion | flops 8388608 | bytes 13631488 | tf_op jit(solution)/shard_map/sub | solution.py:53
  340.3 0.7 copy-done.11
  341.1 0.3 copy-done.13
  341.4 2.6 multiply_subtract_fusion.2
  344.0 0.0 copy-done
  344.0 0.2 convert_reduce_fusion.1
  344.1 0.3 fusion.10
  344.4 0.4 convert_reduce_fusion
  344.8 0.0 copy-start.15
  344.8 0.0 copy-start.16
  344.9 1.0 fusion.25
  345.9 1.8 fusion.9
  347.8 1.3 multiply_subtract_fusion.3
  349.0 0.0 copy-done.19
  349.1 0.6 add_subtract_fusion
  (30 shorter events, 0.1 us)
Async XLA Ops:
  177.3 153.8 %copy-start.1 = (f32[256,2048]{1,0:T(8,128)S(1)}, f32[256,2048]{1,0:T(8,128)}, u32[]{:S(2)}) copy-start(f32[256,2048]{1,0:T(8,128)} %wd_ref.1) | copy-start | bytes 6291460
  177.3 153.8 %copy-start.5 = (f32[256,2048]{1,0:T(8,128)S(1)}, f32[256,2048]{1,0:T(8,128)}, u32[]{:S(2)}) copy-start(f32[256,2048]{1,0:T(8,128)} %param.29) | copy-start | bytes 6291460
  331.1 5.5 %copy-start.2 = (f32[64,8192]{1,0:T(8,128)S(1)}, f32[64,8192]{1,0:T(8,128)}, u32[]{:S(2)}) copy-start(f32[64,8192]{1,0:T(8,128)} %wu_ref.1) | copy-start | bytes 6291460
  331.1 5.5 %copy-start.6 = (f32[64,8192]{1,0:T(8,128)S(1)}, f32[64,8192]{1,0:T(8,128)}, u32[]{:S(2)}) copy-start(f32[64,8192]{1,0:T(8,128)} %param.28) | copy-start | bytes 6291460
  331.2 5.5 %copy-start.7 = (f32[64,8192]{1,0:T(8,128)S(1)}, f32[64,8192]{1,0:T(8,128)}, u32[]{:S(2)}) copy-start(f32[64,8192]{1,0:T(8,128)} %param.33) | copy-start | bytes 6291460
  331.2 5.4 %copy-start.12 = (bf16[64,8192]{1,0:T(8,128)(2,1)S(1)}, bf16[64,8192]{1,0:T(8,128)(2,1)}, u32[]{:S(2)}) copy-start(bf16[64,8192]{1,0:T(8,128)(2,1)} %get-tuple-element.54) | copy-start | bytes 3145732
  336.6 3.7 %copy-start.3 = (f32[64,6144]{1,0:T(8,128)S(1)}, f32[64,6144]{1,0:T(8,128)}, u32[]{:S(2)}) copy-start(f32[64,6144]{1,0:T(8,128)} %wq_ref.1) | copy-start | bytes 4718596
  336.6 3.7 %copy-start.10 = (f32[64,6144]{1,0:T(8,128)S(1)}, f32[64,6144]{1,0:T(8,128)}, u32[]{:S(2)}) copy-start(f32[64,6144]{1,0:T(8,128)} %param.26) | copy-start | bytes 4718596
  336.6 4.4 %copy-start.11 = (f32[64,6144]{1,0:T(8,128)S(1)}, f32[64,6144]{1,0:T(8,128)}, u32[]{:S(2)}) copy-start(f32[64,6144]{1,0:T(8,128)} %param.31) | copy-start | bytes 4718596
  336.7 4.7 %copy-start.13 = (bf16[64,6144]{1,0:T(8,128)(2,1)S(1)}, bf16[64,6144]{1,0:T(8,128)(2,1)}, u32[]{:S(2)}) copy-start(bf16[64,6144]{1,0:T(8,128)(2,1)} %get-tuple-element.52) | copy-start | bytes 2359300
  341.4 2.6 copy-start
  341.4 3.0 copy-start.4
  344.0 1.9 copy-start.8
  344.0 1.9 copy-start.14
  344.8 2.9 copy-start.9
  344.8 2.9 copy-start.15
  344.8 2.9 copy-start.16
  344.9 2.9 copy-start.17
  347.7 1.3 copy-start.18
  347.7 1.3 copy-start.19
  347.7 1.3 copy-start.20
  347.7 1.3 copy-start.21

commit v3 on v1

--- a/solution.py
+++ b/solution.py
@@ -933,6 +933,8 @@
             wu_cut[to, :, part * rows_down : (part + 1) * rows_down] = wu_raw[
                 :, part * width + to * rows_down : part * width + (to + 1) * rows_down
             ].astype(bf16)
+    for copy in cols_u:
+        copy.start()
     keep_u = pltpu.make_async_copy(wu_cut.at[slot], wu_own, local.at[1])
     keep_u.start()
     raw[3].wait()
@@ -999,8 +1001,6 @@
                 norm_rows(shard - dist if side == 0 else shard + dist)
 
     chain_x.step(1)
-    for copy in cols_u:
-        copy.start()
     chain_x.pair(0, 0).wait_recv()
     norm_rows(shard)
     spread_d.relay()

time: 343 us -> 346 us (level)
    pallas_call x1, Pallas kernels: 174 us -> 184 us  [forward_all(): pl.pallas_call(partial(forward_kernel, n_plane, n_shard), out_shape=[shap...]
    pallas_call x1, Pallas kernels: 147 us -> 139 us  [backward_all(): pl.pallas_call(partial(backward_kernel, n_plane, n_shard), out_shape=[sha...]
where the time goes in v3:
time: 346 us; the launch traced here: 344 us
  Pallas kernels  323 us (93%)
  other arithmetic  16.8 us (5%)
  local copies, waits for them, and re-layouts  3.48 us (1%)
    pallas_call x1, Pallas kernels, forward_all(): pl.pallas_call(partial(forward_kernel, n_plane, n_shard), out_shape=[shap...  184 us
    pallas_call x1, Pallas kernels, backward_all(): pl.pallas_call(partial(backward_kernel, n_plane, n_shard), out_shape=[sha...  139 us
    sub x5, other arithmetic, adam_step(): weight - rate * (unbiased / (jnp.sqrt(scaled) + 1e-08) + decay * weight)  13.5 us

profile of v3, /device:TPU:18, one launch (start us, length us, event | category | flops | bytes accessed | tf_op | source)
XLA Modules:
  0.0 344.0 jit_solution(2199201584673692477)
XLA Ops:
  0.7 1.3 pad.8.vec_ref
  2.0 0.6 fusion.19.freq_ref
  2.6 184.2 %forward_all.1 = (bf16[1024,2048]{1,0:T(8,128)(2,1)}, bf16[1024,2048]{1,0:T(8,128)(2,1)}, bf16[1024,2048]{1,0:T(8,128)(2,1)}, bf16[1024,2048]{1,0:T(8,128)(2,1)}...) custom-call(bf16[128,2048]{1,0:T(8,128)(2,1)} %bitcast.17, ...), custom_call_target="tpu_custom_call" | custom-call | tf_op jit(solution)/shard_map/forward_all/pallas_call | solution.py:1287
  186.8 0.0 copy-start.1
  186.8 0.0 copy-start.5
  186.8 138.7 %backward_all.1 = (bf16[128,2048]{1,0:T(8,128)(2,1)}, bf16[128,2048]{1,0:T(8,128)(2,1)}, bf16[64,6144]{1,0:T(8,128)(2,1)}, bf16[64,8192]{1,0:T(8,128)(2,1)}, bf1...) custom-call(bf16[1024,2048]{1,0:T(8,128)(2,1)} %get-tuple-element.37.x_ref, ...), custom_call_target="tpu_custom_call" | custom-call | tf_op jit(solution)/shard_map/backward_all/pallas_call | solution.py:1809
  325.5 0.0 copy-start.2
  325.5 0.0 copy-start.6
  325.5 0.0 copy-start.7
  325.5 5.4 %multiply_subtract_fusion = (f32[256,2048]{1,0:T(8,128)}, f32[256,2048]{1,0:T(8,128)}, f32[256,2048]{1,0:T(8,128)}) fusion(f32[256,2048]{1,0:T(8,128)S(1)} %copy-done.1, f32[256,2048]{1,0:T(8,128)S(1)} %copy-done.5, f32[256,2048]{1,0:T(8,128)} %param.34, bf16[256,2048]{1,0:T(8,128)(2,1)} %get-tuple-element.55), kind=kLoop, calls=%fused_computation.5 | loop fusion | flops 8388608 | bytes 13631488 | tf_op jit(solution)/shard_map/sub | solution.py:53
  331.0 0.0 copy-done.2
  331.0 0.0 copy-start.3
  331.0 0.0 copy-start.10
  331.0 0.0 copy-start.11
  331.0 0.0 copy-start.13
  331.0 3.7 %multiply_subtract_fusion.1 = (f32[64,8192]{1,0:T(8,128)}, f32[64,8192]{1,0:T(8,128)}, f32[64,8192]{1,0:T(8,128)}) fusion(f32[64,8192]{1,0:T(8,128)S(1)} %copy-done.2, f32[64,8192]{1,0:T(8,128)S(1)} %copy-done.6, f32[64,8192]{1,0:T(8,128)S(1)} %copy-done.7, bf16[64,8192]{1,0:T(8,128)(2,1)S(1)} %copy-done.12), kind=kLoop, calls=%fused_computation.6 | loop fusion | flops 8388608 | bytes 13631488 | tf_op jit(solution)/shard_map/sub | solution.py:53
  334.7 0.0 copy-done.10
  334.7 0.7 copy-done.11
  335.4 0.3 copy-done.13
  335.8 2.6 multiply_subtract_fusion.2
  338.3 0.2 convert_reduce_fusion.1
  338.5 0.3 fusion.10
  338.8 0.4 convert_reduce_fusion
  339.2 0.0 copy-start.15
  339.2 0.0 copy-start.16
  339.2 1.0 fusion.25
  340.3 1.8 fusion.9
  342.1 0.0 copy-done.9
  342.1 0.0 copy-done.15
  342.1 0.0 copy-done.16
  342.1 1.3 multiply_subtract_fusion.3
  343.4 0.6 add_subtract_fusion
  (30 shorter events, 0.1 us)
Async XLA Ops:
  186.8 138.7 %copy-start.1 = (f32[256,2048]{1,0:T(8,128)S(1)}, f32[256,2048]{1,0:T(8,128)}, u32[]{:S(2)}) copy-start(f32[256,2048]{1,0:T(8,128)} %wd_ref.1) | copy-start | bytes 6291460
  186.8 138.7 %copy-start.5 = (f32[256,2048]{1,0:T(8,128)S(1)}, f32[256,2048]{1,0:T(8,128)}, u32[]{:S(2)}) copy-start(f32[256,2048]{1,0:T(8,128)} %param.29) | copy-start | bytes 6291460
  325.5 5.5 %copy-start.2 = (f32[64,8192]{1,0:T(8,128)S(1)}, f32[64,8192]{1,0:T(8,128)}, u32[]{:S(2)}) copy-start(f32[64,8192]{1,0:T(8,128)} %wu_ref.1) | copy-start | bytes 6291460
  325.5 5.5 %copy-start.6 = (f32[64,8192]{1,0:T(8,128)S(1)}, f32[64,8192]{1,0:T(8,128)}, u32[]{:S(2)}) copy-start(f32[64,8192]{1,0:T(8,128)} %param.28) | copy-start | bytes 6291460
  325.5 5.5 %copy-start.7 = (f32[64,8192]{1,0:T(8,128)S(1)}, f32[64,8192]{1,0:T(8,128)}, u32[]{:S(2)}) copy-start(f32[64,8192]{1,0:T(8,128)} %param.33) | copy-start | bytes 6291460
  325.5 5.4 %copy-start.12 = (bf16[64,8192]{1,0:T(8,128)(2,1)S(1)}, bf16[64,8192]{1,0:T(8,128)(2,1)}, u32[]{:S(2)}) copy-start(bf16[64,8192]{1,0:T(8,128)(2,1)} %get-tuple-element.54) | copy-start | bytes 3145732
  331.0 3.7 %copy-start.3 = (f32[64,6144]{1,0:T(8,128)S(1)}, f32[64,6144]{1,0:T(8,128)}, u32[]{:S(2)}) copy-start(f32[64,6144]{1,0:T(8,128)} %wq_ref.1) | copy-start | bytes 4718596
  331.0 3.7 %copy-start.10 = (f32[64,6144]{1,0:T(8,128)S(1)}, f32[64,6144]{1,0:T(8,128)}, u32[]{:S(2)}) copy-start(f32[64,6144]{1,0:T(8,128)} %param.26) | copy-start | bytes 4718596
  331.0 4.4 %copy-start.11 = (f32[64,6144]{1,0:T(8,128)S(1)}, f32[64,6144]{1,0:T(8,128)}, u32[]{:S(2)}) copy-start(f32[64,6144]{1,0:T(8,128)} %param.31) | copy-start | bytes 4718596
  331.0 4.7 %copy-start.13 = (bf16[64,6144]{1,0:T(8,128)(2,1)S(1)}, bf16[64,6144]{1,0:T(8,128)(2,1)}, u32[]{:S(2)}) copy-start(bf16[64,6144]{1,0:T(8,128)(2,1)} %get-tuple-element.52) | copy-start | bytes 2359300
  335.7 2.6 copy-start
  335.7 3.0 copy-start.4
  338.3 1.9 copy-start.8
  338.3 1.9 copy-start.14
  339.2 2.9 copy-start.9
  339.2 2.9 copy-start.15
  339.2 2.9 copy-start.16
  339.2 2.9 copy-start.17
  342.1 1.3 copy-start.18
  342.1 1.3 copy-start.19
  342.1 1.3 copy-start.20
  342.1 1.3 copy-start.21
